TPU v7x, 512 devices: a whole 4x8x8 slice. The times are simulated.
512 devices in a mesh: fsdp: 64 (over z, x, core), rep: 8 (over y).
Axes of the slice: x: 4, y: 8, z: 8, core: 2. Of those that a mesh axis runs over, the one named last changes fastest.
Arguments:
- gradients: bfloat16 [8, 16, 256, 8192], P('rep', None, 'fsdp'), may hold values from -0.5 to 0.5
- owned_blocks: int32 [64, 8, 2], replicated, may hold values from 0 to 512, as said below
- rows_valid: int32 [512], replicated, may hold values from 128 to 256
- cols_valid: int32 [512], replicated, may hold values from 128 to 256
- left_factor: float32 [64, 8, 2, 256, 256], P('fsdp', 'rep'), may hold values from -3 to 3
- right_factor: float32 [64, 8, 2, 256, 256], P('fsdp', 'rep'), may hold values from -3 to 3
- left_root: bfloat16 [64, 8, 2, 256, 256], P('fsdp', 'rep'), may hold values from -1 to 3
- right_root: bfloat16 [64, 8, 2, 256, 256], P('fsdp', 'rep'), may hold values from -1 to 3
- second_moment: float32 [64, 8, 2, 256, 256], P('fsdp', 'rep'), may hold values from 0.0001 to 0.01
Outputs:
- update: bfloat16 [16, 256, 8192], P(None, 'fsdp')
- left_new: float32 [64, 8, 2, 256, 256], P('fsdp', 'rep')
- right_new: float32 [64, 8, 2, 256, 256], P('fsdp', 'rep')
Inputs may be any that keep to these rules, and one draw needn't show every extreme that they name: `owned_blocks`: every block id 0 to 511 stands in exactly one slot; the value 512 marks an empty slot; slots of one owner are filled from slot 0; some owners fill all 2 slots and some hold none.
All inputs are finite; a program needn't handle non-finite values.
Results may differ from a plain program's by a relative error of at most 0.02.
Values may be sent and summed in bfloat16 or wider, within the bound.
No kernel may reach another device: no remote copies, remote signals or barrier semaphores. Data moves between devices by JAX's collectives and lax.ppermute only.
A program may use at most 64 MiB of HBM per device.

v0:
```python
import jax
import jax.numpy as jnp
from jax import lax
from jax.sharding import PartitionSpec as P

factor_decay = 0.95
moment_decay = 0.999
adam_eps = 1e-08


def body(
    gradients,
    owned_blocks,
    rows_valid,
    cols_valid,
    left_factor,
    right_factor,
    left_root,
    right_root,
    second_moment,
):
    shards = lax.axis_size("fsdp")
    copies = lax.axis_size("rep")
    shard_index = lax.axis_index("fsdp")
    copy_index = lax.axis_index("rep")
    slab_count, row_count, col_count = (gradients.shape[1], gradients.shape[2], gradients.shape[3])
    size_b = left_factor.shape[-1]
    col_blocks = col_count // size_b
    slot_count = owned_blocks.shape[2]
    block_total = slab_count * col_blocks
    pieces = (
        gradients[0]
        .reshape(slab_count, row_count, col_blocks, size_b)
        .transpose(0, 2, 1, 3)
        .reshape(block_total, row_count, size_b)
    )
    outgoing = jnp.take(pieces, owned_blocks, axis=0, mode="fill", fill_value=0)
    arrived = lax.all_to_all(outgoing, "fsdp", split_axis=0, concat_axis=3, tiled=True)
    totals = lax.psum_scatter(
        arrived[0].astype(jnp.float32).astype(jnp.bfloat16), "rep", scatter_dimension=0, tiled=True
    ).astype(jnp.float32)
    blocks = totals[0].astype(jnp.bfloat16)
    owned_here = owned_blocks[shard_index, copy_index]
    row_limit = jnp.take(rows_valid, owned_here, mode="fill", fill_value=0)
    col_limit = jnp.take(cols_valid, owned_here, mode="fill", fill_value=0)
    row_ids = jnp.arange(size_b, dtype=jnp.int32)
    inside = (row_ids[None, :, None] < row_limit[:, None, None]) & (
        row_ids[None, None, :] < col_limit[:, None, None]
    )
    grad_block = jnp.where(inside, blocks, jnp.zeros((), jnp.bfloat16))
    grad_wide = grad_block.astype(jnp.float32)
    left_next = factor_decay * left_factor[0, 0] + (1.0 - factor_decay) * jnp.einsum(
        "kij,klj->kil", grad_wide, grad_wide, precision=lax.Precision.HIGHEST
    )
    right_next = factor_decay * right_factor[0, 0] + (1.0 - factor_decay) * jnp.einsum(
        "kji,kjl->kil", grad_wide, grad_wide, precision=lax.Precision.HIGHEST
    )
    halfway = jnp.einsum(
        "kij,kjl->kil", left_root[0, 0], grad_block, preferred_element_type=jnp.float32
    ).astype(jnp.bfloat16)
    precond = jnp.einsum(
        "kij,kjl->kil", halfway, right_root[0, 0], preferred_element_type=jnp.float32
    )
    precond = jnp.where(inside, precond, jnp.float32(0.0))
    moment = moment_decay * second_moment[0, 0] + (1.0 - moment_decay) * grad_wide * grad_wide
    adam = grad_wide / (jnp.sqrt(moment) + adam_eps)
    adam_norm = jnp.sqrt(jnp.sum(adam * adam, axis=(1, 2)))
    pre_norm = jnp.sqrt(jnp.sum(precond * precond, axis=(1, 2)) + 1e-06)
    slot_update = (precond * (adam_norm / pre_norm)[:, None, None]).astype(jnp.bfloat16)
    rows_split = slot_update.reshape(slot_count, shards, row_count, size_b)
    everyone = lax.all_gather(rows_split[None], "rep", axis=0, tiled=True)
    returned = lax.all_to_all(everyone, "fsdp", split_axis=2, concat_axis=2, tiled=True)
    arranged = returned.transpose(2, 0, 1, 3, 4).reshape(
        shards * copies * slot_count, row_count, size_b
    )
    slot_ids = owned_blocks.reshape(-1)
    placed = (
        jnp.zeros((block_total, row_count, size_b), jnp.bfloat16)
        .at[slot_ids]
        .set(arranged, mode="drop")
    )
    update = (
        placed.reshape(slab_count, col_blocks, row_count, size_b)
        .transpose(0, 2, 1, 3)
        .reshape(slab_count, row_count, col_count)
    )
    return (update, left_next[None, None], right_next[None, None])


def solution(mesh):
    in_specs = (
        P("rep", None, "fsdp", None),
        P(),
        P(),
        P(),
        P("fsdp", "rep", None, None, None),
        P("fsdp", "rep", None, None, None),
        P("fsdp", "rep", None, None, None),
        P("fsdp", "rep", None, None, None),
        P("fsdp", "rep", None, None, None),
    )
    out_specs = (
        P(None, "fsdp", None),
        P("fsdp", "rep", None, None, None),
        P("fsdp", "rep", None, None, None),
    )
    return jax.shard_map(body, mesh=mesh, in_specs=in_specs, out_specs=out_specs, check_vma=False)
```

profile of v0, /device:TPU:6, one launch (start us, length us, event | category | flops | bytes accessed | tf_op | source)
XLA Modules:
  0.0 279.4 jit_solution(13364112744980480520)
XLA Ops:
  7.2 0.7 compare_select_fusion
  8.0 0.7 compare_and_fusion
  8.7 1.8 reshape.166
  10.6 0.8 copy.26
  11.9 3.9 %gather_fusion = bf16[1024,4,256]{2,1,0:T(4,128)(2,1)S(1)} fusion(bf16[512,4,256]{2,1,0:T(4,128)(2,1)S(1)} %copy.26, s32[1024]{0:T(1024)S(1)} %broadcast_clamp_fusion), kind=kCustom, calls=%fused_computation.2 | custom fusion | bytes 4198400 | tf_op jit(solution)/shard_map/jit(_take)/gather | solution.py:37
  15.9 1.7 broadcast_select_fusion
  17.6 64.9 %all_to_all.20 = bf16[64,8,2,4,256]{4,3,2,1,0:T(4,128)(2,1)S(1)} all-to-all(bf16[64,8,2,4,256]{4,3,2,1,0:T(4,128)(2,1)S(1)} %broadcast_select_fusion), channel_id=1, replica_groups=mesh['fsdp'=64,'rep'=8] {'fsdp'}, dimensions={0} | all-to-all | bytes 4194304 | tf_op jit(solution)/shard_map/all_to_all | solution.py:38
  82.5 1.0 copy.27
  83.4 2.1 squeeze.17
  85.6 0.6 copy-done.6
  86.4 0.6 gather_fusion.1
  87.1 0.6 gather_fusion.2
  87.8 38.4 %reduce-scatter.2.cloned.1.call-done = bf16[1,2,256,256]{3,2,1,0:T(8,128)(2,1)} async-done(((bf16[8,2,256,256]{3,2,1,0:T(8,128)(2,1)}), bf16[1,2,256,256]{3,2,1,0:T(8,128)(2,1)}) %reduce-scatter.2.cloned.1.call-update) | async-done | bytes 262160 | tf_op jit(solution)/shard_map/reduce_scatter | solution.py:39
  126.2 1.5 fusion.8
  127.7 1.7 multiply_reduce_fusion
  129.5 0.8 copy.30
  130.4 49.3 %all-gather.2.cloned.1.call-done = bf16[8,2,64,4,256]{4,3,1,0,2:T(4,128)(2,1)} async-done(((bf16[1,2,64,4,256]{4,3,1,0,2:T(4,128)(2,1)}), bf16[8,2,64,4,256]{4,3,1,0,2:T(4,128)(2,1)}) %all-gather.2.cloned.1.call-update) | async-done | bytes 2097168 | tf_op jit(solution)/shard_map/all_gather | solution.py:71
  179.6 10.9 %all-to-all-start.1 = ((bf16[8,2,64,4,256]{4,3,1,0,2:T(4,128)(2,1)}), bf16[8,2,64,4,256]{4,3,1,0,2:T(4,128)(2,1)S(1)}, u32[]{:S(2)}, u32[]{:S(2)}) async-start(bf16[8,2,64,4,256]{4,3,1,0,2:T(4,128)(2,1)} %all-gather.2.cloned.1.call-done), calls=%async_computation.2 | async-start | bytes 4194304 | tf_op jit(solution)/shard_map/all_to_all | solution.py:72
  190.9 1.2 fusion.1
  192.2 2.2 fusion.3
  194.4 47.5 %all-to-all-done.1 = bf16[8,2,64,4,256]{4,3,1,0,2:T(4,128)(2,1)S(1)} async-done(((bf16[8,2,64,4,256]{4,3,1,0,2:T(4,128)(2,1)}), bf16[8,2,64,4,256]{4,3,1,0,2:T(4,128)(2,1)S(1)}, u32[]{:S(2)}, u32[]{:S(2)}) %all-to-all-start.1) | async-done | bytes 2097184 | tf_op jit(solution)/shard_map/all_to_all | solution.py:72
  242.1 27.9 %scatter_fusion = bf16[512,4,256]{2,1,0:T(4,128)(2,1)S(1)} fusion(bf16[512,4,256]{2,1,0:T(4,128)(2,1)S(1)} %broadcast_in_dim.38, s32[1024]{0:T(1024)S(1)} %bitcast.56, bf16[1024,4,256]{2,1,0:T(4,128)(2,1)S(1)} %bitcast.53), kind=kCustom, calls=%fused_computation.3 | custom fusion | bytes 6295552 | tf_op jit(solution)/shard_map/scatter | solution.py:80
  270.2 0.5 reshape.125
  270.7 1.8 copy.33
  (37 shorter events, 2.0 us)
Async XLA Ops:
  7.2 120.5 %copy-start = (bf16[1,1,2,256,256]{4,3,2,1,0:T(8,128)(2,1)S(1)}, bf16[1,1,2,256,256]{4,3,2,1,0:T(8,128)(2,1)}, u32[]{:S(2)}) copy-start(bf16[1,1,2,256,256]{4,3,2,1,0:T(8,128)(2,1)} %param.18) | copy-start | bytes 786436
  7.2 119.0 %reduce-scatter.2.cloned.1.call-start = ((), (), s32[]{:S(2)}) async-start(), calls=%async_computation.3 | async-start | bytes 2359296 | tf_op jit(solution)/shard_map/reduce_scatter | solution.py:39
  85.5 0.7 copy-start.6
  85.5 0.9 copy-start.1
  85.5 1.5 copy-start.2
  85.5 40.7 %copy-start.5 = (f32[1,1,2,256,256]{4,3,2,1,0:T(8,128)S(1)}, f32[1,1,2,256,256]{4,3,2,1,0:T(8,128)}, u32[]{:S(2)}) copy-start(f32[1,1,2,256,256]{4,3,2,1,0:T(8,128)} %param.19) | copy-start | bytes 1572868
  85.5 42.1 %copy-start.7 = (bf16[1,1,2,256,256]{4,3,2,1,0:T(8,128)(2,1)S(1)}, bf16[1,1,2,256,256]{4,3,2,1,0:T(8,128)(2,1)}, u32[]{:S(2)}) copy-start(bf16[1,1,2,256,256]{4,3,2,1,0:T(8,128)(2,1)} %param.17) | copy-start | bytes 786436
  85.6 94.1 %all-gather.2.cloned.1.call-start = ((), (), s32[]{:S(2)}) async-start(), calls=%async_computation.4 | async-start | bytes 2359296 | tf_op jit(solution)/shard_map/all_gather | solution.py:71
  130.4 60.6 %copy-start.3 = (bf16[1,2,256,256]{3,2,1,0:T(8,128)(2,1)S(1)}, bf16[1,2,256,256]{3,2,1,0:T(8,128)(2,1)}, u32[]{:S(2)}) copy-start(bf16[1,2,256,256]{3,2,1,0:T(8,128)(2,1)} %reduce-scatter.2.cloned.1.call-done) | copy-start | bytes 786436
  130.4 60.6 %copy-start.4 = (f32[1,1,2,256,256]{4,3,2,1,0:T(8,128)S(1)}, f32[1,1,2,256,256]{4,3,2,1,0:T(8,128)}, u32[]{:S(2)}) copy-start(f32[1,1,2,256,256]{4,3,2,1,0:T(8,128)} %param.16) | copy-start | bytes 1572868
  179.6 62.2 %all-to-all-start.1 = ((bf16[8,2,64,4,256]{4,3,1,0,2:T(4,128)(2,1)}), bf16[8,2,64,4,256]{4,3,1,0,2:T(4,128)(2,1)S(1)}, u32[]{:S(2)}, u32[]{:S(2)}) async-start(bf16[8,2,64,4,256]{4,3,1,0,2:T(4,128)(2,1)} %all-gather.2.cloned.1.call-done), calls=%async_computation.2 | async-start | bytes 4194304 | tf_op jit(solution)/shard_map/all_to_all | solution.py:72
Sparse Core Ops, SparseCore 0:
  85.7 40.4 reduce-scatter.1
  130.5 49.1 all-gather.1
where the time goes:
time: 280 us; the launch traced here: 279 us
  waiting for transfers between devices  135 us (48%)
  blocking collectives  64.9 us (23%)
  local copies, waits for them, and re-layouts  44.2 us (16%)
  between operations  14.2 us (5%)
  starting transfers between devices  11 us (4%)
  matrix products  5.1 us (2%)
  other arithmetic  4.8 us (2%)
    all_to_all x1, blocking collectives, body(): lax.all_to_all(outgoing, 'fsdp', split_axis=0, concat_axis=3, tiled=True)  64.9 us
    all_gather x1, waiting for transfers between devices, body(): everyone = lax.all_gather(rows_split[None], 'rep', axis=0, tiled=True)  49.3 us
    all_to_all x1, waiting for transfers between devices, body(): lax.all_to_all(everyone, 'fsdp', split_axis=2, concat_axis=2, tiled=True)  47.5 us
    reduce_scatter x1, waiting for transfers between devices, body(): lax.psum_scatter(arrived[0].astype(jnp.float32).astype(jnp.bfloat16), 're...  38.4 us
    scatter x2, local copies, waits for them, and re-layouts, body(): placed = jnp.zeros((block_total, row_count, size_b), jnp.bfloat16).at[slo...  28.1 us
    all_to_all x1, starting transfers between devices, body(): lax.all_to_all(everyone, 'fsdp', split_axis=2, concat_axis=2, tiled=True)  10.9 us
  transfers between devices with their start and end apart: 3, of which 3 were waited for; matrix products, arithmetic and copies ran while one was open for 2% of the time, Pallas kernels for 0%

commit v1 on v0

v1 whole, which is shorter than its diff:
```python
import jax
import jax.numpy as jnp
from jax import lax
from jax.sharding import PartitionSpec as P

factor_decay = 0.95
moment_decay = 0.999
adam_eps = 1e-08


def body(
    gradients,
    owned_blocks,
    rows_valid,
    cols_valid,
    left_factor,
    right_factor,
    left_root,
    right_root,
    second_moment,
):
    shards = lax.axis_size("fsdp")
    copies = lax.axis_size("rep")
    owners = shards * copies
    shard_index = lax.axis_index("fsdp")
    copy_index = lax.axis_index("rep")
    slab_count, row_count, col_count = gradients.shape[1:]
    size_b = left_factor.shape[-1]
    col_blocks = col_count // size_b
    slot_count = owned_blocks.shape[2]
    block_total = slab_count * col_blocks

    def shifted(operand, by):
        return lax.ppermute(operand, "rep", [(i, (i + by) % copies) for i in range(copies)])

    def crossed(operand, by):
        pairs = []
        for owner in range(shards):
            step = by if owner % 2 == 0 else -by
            pairs += [
                (owner * copies + i, owner * copies + (i + step) % copies) for i in range(copies)
            ]
        return lax.ppermute(operand, ("fsdp", "rep"), pairs)

    rows = (
        gradients[0]
        .reshape(slab_count, row_count, col_blocks, size_b)
        .transpose(1, 0, 2, 3)
        .reshape(row_count, block_total, size_b)
    )

    def row_at(by):
        return lax.dynamic_index_in_dim(rows, (copy_index + by) % row_count, 0, keepdims=False)

    from_two = crossed(row_at(2), 2)
    from_left = shifted(row_at(1), 1)
    from_right = shifted(row_at(3), -1)
    summed = lax.optimization_barrier(
        (
            row_at(0).astype(jnp.float32)
            + from_left.astype(jnp.float32)
            + from_right.astype(jnp.float32)
            + from_two.astype(jnp.float32)
        ).astype(jnp.bfloat16)
    )
    slot_ids = owned_blocks.reshape(-1)
    block_ids = jnp.arange(block_total, dtype=jnp.int32)
    pick = (slot_ids[:, None] == block_ids[None, :]).astype(jnp.bfloat16)
    outgoing = (
        jnp.dot(pick, summed, preferred_element_type=jnp.float32)
        .astype(jnp.bfloat16)
        .reshape(owners, slot_count, size_b)
    )
    mine = lax.all_to_all(outgoing, ("fsdp", "rep"), split_axis=0, concat_axis=0, tiled=True)
    blocks = (
        mine.reshape(shards, copies // row_count, row_count, slot_count, size_b)
        .astype(jnp.float32)
        .sum(axis=1)
        .transpose(2, 0, 1, 3)
        .reshape(slot_count, size_b, size_b)
        .astype(jnp.bfloat16)
    )
    owned_here = owned_blocks[shard_index, copy_index]
    row_limit = jnp.take(rows_valid, owned_here, mode="fill", fill_value=0)
    col_limit = jnp.take(cols_valid, owned_here, mode="fill", fill_value=0)
    row_ids = jnp.arange(size_b, dtype=jnp.int32)
    inside = (row_ids[None, :, None] < row_limit[:, None, None]) & (
        row_ids[None, None, :] < col_limit[:, None, None]
    )
    grad_block = jnp.where(inside, blocks, jnp.zeros((), jnp.bfloat16))
    grad_wide = grad_block.astype(jnp.float32)
    left_next = factor_decay * left_factor[0, 0] + (1.0 - factor_decay) * jnp.einsum(
        "kij,klj->kil", grad_block, grad_block, preferred_element_type=jnp.float32
    )
    right_next = factor_decay * right_factor[0, 0] + (1.0 - factor_decay) * jnp.einsum(
        "kji,kjl->kil", grad_block, grad_block, preferred_element_type=jnp.float32
    )
    halfway = jnp.einsum(
        "kij,kjl->kil", left_root[0, 0], grad_block, preferred_element_type=jnp.float32
    ).astype(jnp.bfloat16)
    precond = jnp.einsum(
        "kij,kjl->kil", halfway, right_root[0, 0], preferred_element_type=jnp.float32
    )
    precond = jnp.where(inside, precond, jnp.float32(0.0))
    moment = moment_decay * second_moment[0, 0] + (1.0 - moment_decay) * grad_wide * grad_wide
    adam = grad_wide / (jnp.sqrt(moment) + adam_eps)
    adam_norm = jnp.sqrt(jnp.sum(adam * adam, axis=(1, 2)))
    pre_norm = jnp.sqrt(jnp.sum(precond * precond, axis=(1, 2)) + 1e-06)
    slot_update = (precond * (adam_norm / pre_norm)[:, None, None]).astype(jnp.bfloat16)
    by_row = slot_update.reshape(slot_count, shards, 1, row_count, size_b).transpose(1, 2, 3, 0, 4)
    parts_out = jnp.broadcast_to(
        by_row, (shards, copies // row_count, row_count, slot_count, size_b)
    ).reshape(owners, slot_count, size_b)
    returned = lax.all_to_all(parts_out, ("fsdp", "rep"), split_axis=0, concat_axis=0, tiled=True)
    place = (block_ids[:, None] == slot_ids[None, :]).astype(jnp.bfloat16)
    placed = jnp.dot(
        place, returned.reshape(owners * slot_count, size_b), preferred_element_type=jnp.float32
    ).astype(jnp.bfloat16)
    row_two = crossed(placed, 2)
    row_one = shifted(placed, -1)
    row_three = shifted(placed, 1)
    gathered = jnp.zeros((row_count, block_total, size_b), jnp.bfloat16)
    for by, entries in enumerate((placed, row_one, row_two, row_three)):
        gathered = lax.dynamic_update_index_in_dim(
            gathered, entries, (copy_index + by) % row_count, 0
        )
    update = (
        gathered.reshape(row_count, slab_count, col_blocks, size_b)
        .transpose(1, 0, 2, 3)
        .reshape(slab_count, row_count, col_count)
    )
    return (update, left_next[None, None], right_next[None, None])


def solution(mesh):
    in_specs = (
        P("rep", None, "fsdp", None),
        P(),
        P(),
        P(),
        P("fsdp", "rep", None, None, None),
        P("fsdp", "rep", None, None, None),
        P("fsdp", "rep", None, None, None),
        P("fsdp", "rep", None, None, None),
        P("fsdp", "rep", None, None, None),
    )
    out_specs = (
        P(None, "fsdp", None),
        P("fsdp", "rep", None, None, None),
        P("fsdp", "rep", None, None, None),
    )
    return jax.shard_map(body, mesh=mesh, in_specs=in_specs, out_specs=out_specs, check_vma=False)
```

time: 280 us -> 129 us (0.46)
  waiting for transfers between devices: 135 us -> 39.5 us
  local copies, waits for them, and re-layouts: 44.2 us -> 9.54 us
  blocking collectives: 64.9 us -> 31.7 us
  starting transfers between devices: 11 us -> 38.6 us
  between operations: 14.2 us -> 1.02 us
    all_gather x1 -> x0, waiting for transfers between devices: 49.3 us -> none  [body(): everyone = lax.all_gather(rows_split[None], 'rep', axis=0, tiled=True)]
    reduce_scatter x1 -> x0, waiting for transfers between devices: 38.4 us -> none  [body(): lax.psum_scatter(arrived[0].astype(jnp.float32).astype(jnp.bfloat16), 're...]
    all_to_all x1, blocking collectives: 64.9 us -> 31.7 us  [body(): lax.all_to_all(parts_out, ('fsdp', 'rep'), split_axis=0, concat_axis=0, t...]
    all_to_all x1, waiting for transfers between devices: 47.5 us -> 18.6 us  [body(): lax.all_to_all(outgoing, ('fsdp', 'rep'), split_axis=0, concat_axis=0, ti...]
    scatter x2 -> x0, local copies, waits for them, and re-layouts: 28.1 us -> none  [body(): placed = jnp.zeros((block_total, row_count, size_b), jnp.bfloat16).at[slo...]
    ppermute x0 -> x6, waiting for transfers between devices: none -> 20.9 us  [the longest x2 12.8 us: crossed(): return lax.ppermute(operand, ('fsdp', 'rep'), pairs)]
    ppermute x0 -> x6, starting transfers between devices: none -> 19.2 us  [the longest x4 12.8 us: shifted(): lax.ppermute(operand, 'rep', [(i, (i + by) % copies) for i in range(copie...]
    all_to_all x1, starting transfers between devices: 10.9 us -> 19.4 us  [body(): lax.all_to_all(outgoing, ('fsdp', 'rep'), split_axis=0, concat_axis=0, ti...]
  transfers between devices with their start and end apart: 3 -> 7, of which waited for: 3 -> 7; matrix products, arithmetic and copies ran while one was open for 2% -> 4% of each run, Pallas kernels for 0% -> 0%
where the time goes in v1:
time: 129 us; the launch traced here: 127 us
  waiting for transfers between devices  39.5 us (31%)
  starting transfers between devices  38.6 us (30%)
  blocking collectives  31.7 us (25%)
  local copies, waits for them, and re-layouts  9.54 us (7%)
  matrix products  4.1 us (3%)
  other arithmetic  2.96 us (2%)
    all_to_all x1, blocking collectives, body(): lax.all_to_all(parts_out, ('fsdp', 'rep'), split_axis=0, concat_axis=0, t...  31.7 us
    all_to_all x1, starting transfers between devices, body(): lax.all_to_all(outgoing, ('fsdp', 'rep'), split_axis=0, concat_axis=0, ti...  19.4 us
    all_to_all x1, waiting for transfers between devices, body(): lax.all_to_all(outgoing, ('fsdp', 'rep'), split_axis=0, concat_axis=0, ti...  18.6 us
    ppermute x2, waiting for transfers between devices, crossed(): return lax.ppermute(operand, ('fsdp', 'rep'), pairs)  12.8 us
    ppermute x4, starting transfers between devices, shifted(): lax.ppermute(operand, 'rep', [(i, (i + by) % copies) for i in range(copie...  12.8 us
    ppermute x4, waiting for transfers between devices, shifted(): lax.ppermute(operand, 'rep', [(i, (i + by) % copies) for i in range(copie...  8.06 us
    ppermute x2, starting transfers between devices, crossed(): return lax.ppermute(operand, ('fsdp', 'rep'), pairs)  6.45 us
  transfers between devices with their start and end apart: 7, of which 7 were waited for; matrix products, arithmetic and copies ran while one was open for 4% of the time, Pallas kernels for 0%

profile of v1, /device:TPU:6, one launch (start us, length us, event | category | flops | bytes accessed | tf_op | source)
XLA Modules:
  0.0 127.4 jit_solution(5355683815056916475)
XLA Ops:
  0.7 1.8 %reshape.138 = bf16[16,4,32,256]{3,2,1,0:T(8,128)(2,1)S(1)} reshape(bf16[1,16,4,8192]{3,2,1,0:T(4,128)(2,1)} %param.11) | data formatting | bytes 2097152 | tf_op jit(solution)/shard_map/reshape;squeeze | solution.py:47
  2.7 0.8 dynamic-slice_bitcast_fusion.2
  3.4 3.5 %collective-permute-start = (bf16[512,256]{1,0:T(8,128)(2,1)}, bf16[512,256]{1,0:T(8,128)(2,1)S(1)}, u32[]{:S(2)}, u32[]{:S(2)}) collective-permute-start(bf16[512,256]{1,0:T(8,128)(2,1)} %get-tuple-element.16), channel_id=1, source_target_pairs={{0,1},{1,2},{2,3},{3,4},{4,5},{5,6},{6,7},{7,0},{8,9},{9,10},{10,1... | collective-permute-start | bytes 786440 | tf_op jit(solution)/shard_map/ppermute | solution.py:34
  6.9 3.8 %collective-permute-start.1 = (bf16[512,256]{1,0:T(8,128)(2,1)S(1)}, bf16[512,256]{1,0:T(8,128)(2,1)S(1)}, u32[]{:S(2)}, u32[]{:S(2)}) collective-permute-start(bf16[512,256]{1,0:T(8,128)(2,1)S(1)} %get-tuple-element.18), channel_id=1, source_target_pairs={{0,7},{1,0},{2,1},{3,2},{4,3},{5,4},{6,5},{7,6},{8,15},{9,8},{10,9... | collective-permute-start | bytes 786440 | tf_op jit(solution)/shard_map/ppermute | solution.py:34
  10.7 3.0 %collective-permute-start.2 = (bf16[512,256]{1,0:T(8,128)(2,1)S(1)}, bf16[512,256]{1,0:T(8,128)(2,1)}, u32[]{:S(2)}, u32[]{:S(2)}) collective-permute-start(bf16[512,256]{1,0:T(8,128)(2,1)S(1)} %get-tuple-element.17), channel_id=1, source_target_pairs={{0,2},{1,3},{2,4},{3,5},{4,6},{5,7},{6,0},{7,1},{8,14},{9,15},{10,... | collective-permute-start | bytes 786440 | tf_op jit(solution)/shard_map/ppermute | solution.py:43
  14.4 0.9 collective-permute-done
  15.3 3.6 %collective-permute-done.1 = bf16[512,256]{1,0:T(8,128)(2,1)S(1)} collective-permute-done((bf16[512,256]{1,0:T(8,128)(2,1)S(1)}, bf16[512,256]{1,0:T(8,128)(2,1)S(1)}, u32[]{:S(2)}, u32[]{:S(2)}) %collective-permute-start.1) | collective-permute-done | bytes 262176 | tf_op jit(solution)/shard_map/ppermute | solution.py:34
  18.9 5.2 %collective-permute-done.2 = bf16[512,256]{1,0:T(8,128)(2,1)} collective-permute-done((bf16[512,256]{1,0:T(8,128)(2,1)S(1)}, bf16[512,256]{1,0:T(8,128)(2,1)}, u32[]{:S(2)}, u32[]{:S(2)}) %collective-permute-start.2) | collective-permute-done | bytes 262176 | tf_op jit(solution)/shard_map/ppermute | solution.py:43
  24.1 1.1 fusion.16
  25.7 1.0 reshape.109
  26.7 19.4 %all-to-all-start = ((bf16[512,2,256]{2,1,0:T(2,128)(2,1)}), bf16[512,2,256]{2,1,0:T(2,128)(2,1)S(1)}, u32[]{:S(2)}, u32[]{:S(2)}) async-start(bf16[512,2,256]{2,1,0:T(2,128)(2,1)} %reshape.109), calls=%async_computation | async-start | bytes 1048576 | tf_op jit(solution)/shard_map/all_to_all | solution.py:74
  46.7 0.6 gather_fusion.1
  48.0 18.6 %all-to-all-done = bf16[512,2,256]{2,1,0:T(2,128)(2,1)S(1)} async-done(((bf16[512,2,256]{2,1,0:T(2,128)(2,1)}), bf16[512,2,256]{2,1,0:T(2,128)(2,1)S(1)}, u32[]{:S(2)}, u32[]{:S(2)}) %all-to-all-start) | async-done | bytes 524320 | tf_op jit(solution)/shard_map/all_to_all | solution.py:74
  66.6 0.9 reduce.1
  68.5 0.7 multiply_reduce_fusion
  70.0 31.7 %all_to_all.10 = bf16[512,2,256]{2,1,0:T(2,128)(2,1)S(1)} all-to-all(bf16[512,2,256]{2,1,0:T(2,128)(2,1)S(1)} %bitcast.68), channel_id=1, replica_groups=mesh['fsdp'=64,'rep'=8] {'fsdp','rep'}, dimensions={0} | all-to-all | bytes 1048576 | tf_op jit(solution)/shard_map/all_to_all | solution.py:114
  102.5 2.9 %collective-permute-start.3 = (bf16[512,256]{1,0:T(8,128)(2,1)S(1)}, bf16[512,256]{1,0:T(8,128)(2,1)S(1)}, u32[]{:S(2)}, u32[]{:S(2)}) collective-permute-start(bf16[512,256]{1,0:T(8,128)(2,1)S(1)} %get-tuple-element.24), channel_id=1, source_target_pairs={{0,7},{1,0},{2,1},{3,2},{4,3},{5,4},{6,5},{7,6},{8,15},{9,8},{10,9... | collective-permute-start | bytes 786440 | tf_op jit(solution)/shard_map/ppermute | solution.py:34
  105.4 1.1 fusion.6
  106.5 3.4 %collective-permute-start.4 = (bf16[512,256]{1,0:T(8,128)(2,1)S(1)}, bf16[512,256]{1,0:T(8,128)(2,1)S(1)}, u32[]{:S(2)}, u32[]{:S(2)}) collective-permute-start(bf16[512,256]{1,0:T(8,128)(2,1)S(1)} %get-tuple-element.24), channel_id=1, source_target_pairs={{0,2},{1,3},{2,4},{3,5},{4,6},{5,7},{6,0},{7,1},{8,14},{9,15},{10,... | collective-permute-start | bytes 786440 | tf_op jit(solution)/shard_map/ppermute | solution.py:43
  110.0 1.2 fusion.4
  111.2 2.6 %collective-permute-start.5 = (bf16[512,256]{1,0:T(8,128)(2,1)S(1)}, bf16[512,256]{1,0:T(8,128)(2,1)S(1)}, u32[]{:S(2)}, u32[]{:S(2)}) collective-permute-start(bf16[512,256]{1,0:T(8,128)(2,1)S(1)} %get-tuple-element.24), channel_id=1, source_target_pairs={{0,1},{1,2},{2,3},{3,4},{4,5},{5,6},{6,7},{7,0},{8,9},{9,10},{10,1... | collective-permute-start | bytes 786440 | tf_op jit(solution)/shard_map/ppermute | solution.py:34
  114.0 7.6 %collective-permute-done.4 = bf16[512,256]{1,0:T(8,128)(2,1)S(1)} collective-permute-done((bf16[512,256]{1,0:T(8,128)(2,1)S(1)}, bf16[512,256]{1,0:T(8,128)(2,1)S(1)}, u32[]{:S(2)}, u32[]{:S(2)}) %collective-permute-start.4) | collective-permute-done | bytes 262176 | tf_op jit(solution)/shard_map/ppermute | solution.py:43
  121.6 3.4 %collective-permute-done.5 = bf16[512,256]{1,0:T(8,128)(2,1)S(1)} collective-permute-done((bf16[512,256]{1,0:T(8,128)(2,1)S(1)}, bf16[512,256]{1,0:T(8,128)(2,1)S(1)}, u32[]{:S(2)}, u32[]{:S(2)}) %collective-permute-start.5) | collective-permute-done | bytes 262176 | tf_op jit(solution)/shard_map/ppermute | solution.py:34
  125.6 1.8 %copy.47 = bf16[16,4,8192]{2,1,0:T(4,128)(2,1)} copy(bf16[16,4,8192]{2,0,1:T(8,128)(2,1)S(1)} %reshape.114) | data formatting | bytes 2097152
  (47 shorter events, 5.7 us)
Async XLA Ops:
  0.6 67.8 %copy-start = (bf16[1,1,2,256,256]{4,3,2,1,0:T(8,128)(2,1)S(1)}, bf16[1,1,2,256,256]{4,3,2,1,0:T(8,128)(2,1)}, u32[]{:S(2)}) copy-start(bf16[1,1,2,256,256]{4,3,2,1,0:T(8,128)(2,1)} %param.18) | copy-start | bytes 786436
  2.6 11.2 %copy-start.6 = (s32[64,8,2]{0,2,1:T(2,128)S(1)}, s32[64,8,2]{0,2,1:T(2,128)}, u32[]{:S(2)}) copy-start(s32[64,8,2]{0,2,1:T(2,128)} %param.12) | copy-start | bytes 12292
  2.6 11.7 %copy-start.5 = (f32[1,1,2,256,256]{4,3,2,1,0:T(8,128)S(1)}, f32[1,1,2,256,256]{4,3,2,1,0:T(8,128)}, u32[]{:S(2)}) copy-start(f32[1,1,2,256,256]{4,3,2,1,0:T(8,128)} %param.19) | copy-start | bytes 1572868
  3.4 11.9 %collective-permute-start = (bf16[512,256]{1,0:T(8,128)(2,1)}, bf16[512,256]{1,0:T(8,128)(2,1)S(1)}, u32[]{:S(2)}, u32[]{:S(2)}) collective-permute-start(bf16[512,256]{1,0:T(8,128)(2,1)} %get-tuple-element.16), channel_id=1, source_target_pairs={{0,1},{1,2},{2,3},{3,4},{4,5},{5,6},{6,7},{7,0},{8,9},{9,10},{10,1... | collective-permute-start | bytes 786440 | tf_op jit(solution)/shard_map/ppermute | solution.py:34
  6.9 12.0 %collective-permute-start.1 = (bf16[512,256]{1,0:T(8,128)(2,1)S(1)}, bf16[512,256]{1,0:T(8,128)(2,1)S(1)}, u32[]{:S(2)}, u32[]{:S(2)}) collective-permute-start(bf16[512,256]{1,0:T(8,128)(2,1)S(1)} %get-tuple-element.18), channel_id=1, source_target_pairs={{0,7},{1,0},{2,1},{3,2},{4,3},{5,4},{6,5},{7,6},{8,15},{9,8},{10,9... | collective-permute-start | bytes 786440 | tf_op jit(solution)/shard_map/ppermute | solution.py:34
  10.7 13.3 %collective-permute-start.2 = (bf16[512,256]{1,0:T(8,128)(2,1)S(1)}, bf16[512,256]{1,0:T(8,128)(2,1)}, u32[]{:S(2)}, u32[]{:S(2)}) collective-permute-start(bf16[512,256]{1,0:T(8,128)(2,1)S(1)} %get-tuple-element.17), channel_id=1, source_target_pairs={{0,2},{1,3},{2,4},{3,5},{4,6},{5,7},{6,0},{7,1},{8,14},{9,15},{10,... | collective-permute-start | bytes 786440 | tf_op jit(solution)/shard_map/ppermute | solution.py:43
  25.7 20.4 %copy-start.1 = (s32[512]{0:T(512)S(1)}, s32[512]{0:T(512)}, u32[]{:S(2)}) copy-start(s32[512]{0:T(512)} %param.13) | copy-start | bytes 6148
  26.7 20.1 %copy-start.2 = (s32[512]{0:T(512)S(1)}, s32[512]{0:T(512)}, u32[]{:S(2)}) copy-start(s32[512]{0:T(512)} %param.14) | copy-start | bytes 6148
  26.7 40.0 %all-to-all-start = ((bf16[512,2,256]{2,1,0:T(2,128)(2,1)}), bf16[512,2,256]{2,1,0:T(2,128)(2,1)S(1)}, u32[]{:S(2)}, u32[]{:S(2)}) async-start(bf16[512,2,256]{2,1,0:T(2,128)(2,1)} %reshape.109), calls=%async_computation | async-start | bytes 1048576 | tf_op jit(solution)/shard_map/all_to_all | solution.py:74
  67.6 1.0 copy-start.7
  102.0 3.4 %copy-start.3 = (f32[1,1,2,256,256]{4,3,2,1,0:T(8,128)S(1)}, f32[1,1,2,256,256]{4,3,2,1,0:T(8,128)}, u32[]{:S(2)}) copy-start(f32[1,1,2,256,256]{4,3,2,1,0:T(8,128)} %param.15) | copy-start | bytes 1572868
  102.5 7.5 %copy-start.4 = (f32[1,1,2,256,256]{4,3,2,1,0:T(8,128)S(1)}, f32[1,1,2,256,256]{4,3,2,1,0:T(8,128)}, u32[]{:S(2)}) copy-start(f32[1,1,2,256,256]{4,3,2,1,0:T(8,128)} %param.16) | copy-start | bytes 1572868
  102.5 11.5 %collective-permute-start.3 = (bf16[512,256]{1,0:T(8,128)(2,1)S(1)}, bf16[512,256]{1,0:T(8,128)(2,1)S(1)}, u32[]{:S(2)}, u32[]{:S(2)}) collective-permute-start(bf16[512,256]{1,0:T(8,128)(2,1)S(1)} %get-tuple-element.24), channel_id=1, source_target_pairs={{0,7},{1,0},{2,1},{3,2},{4,3},{5,4},{6,5},{7,6},{8,15},{9,8},{10,9... | collective-permute-start | bytes 786440 | tf_op jit(solution)/shard_map/ppermute | solution.py:34
  106.5 15.1 %collective-permute-start.4 = (bf16[512,256]{1,0:T(8,128)(2,1)S(1)}, bf16[512,256]{1,0:T(8,128)(2,1)S(1)}, u32[]{:S(2)}, u32[]{:S(2)}) collective-permute-start(bf16[512,256]{1,0:T(8,128)(2,1)S(1)} %get-tuple-element.24), channel_id=1, source_target_pairs={{0,2},{1,3},{2,4},{3,5},{4,6},{5,7},{6,0},{7,1},{8,14},{9,15},{10,... | collective-permute-start | bytes 786440 | tf_op jit(solution)/shard_map/ppermute | solution.py:43
  111.2 13.9 %collective-permute-start.5 = (bf16[512,256]{1,0:T(8,128)(2,1)S(1)}, bf16[512,256]{1,0:T(8,128)(2,1)S(1)}, u32[]{:S(2)}, u32[]{:S(2)}) collective-permute-start(bf16[512,256]{1,0:T(8,128)(2,1)S(1)} %get-tuple-element.24), channel_id=1, source_target_pairs={{0,1},{1,2},{2,3},{3,4},{4,5},{5,6},{6,7},{7,0},{8,9},{9,10},{10,1... | collective-permute-start | bytes 786440 | tf_op jit(solution)/shard_map/ppermute | solution.py:34

commit v2 on v0

v2 whole, which is shorter than its diff:
```python
import functools

import jax
import jax.numpy as jnp
from jax import lax
from jax.experimental import pallas as pl
from jax.experimental.pallas import tpu as pltpu
from jax.sharding import PartitionSpec as P

factor_decay = 0.95
moment_decay = 0.999
adam_eps = 1e-08
LANES = 128
BF16 = jnp.bfloat16
F32 = jnp.float32


def call(kernel, out_shape, scratch_shapes, in_spaces, out_space=pltpu.VMEM, limit=32 * 1024 * 1024):
    return pl.pallas_call(
        kernel,
        out_shape=out_shape,
        in_specs=[pl.BlockSpec(memory_space=space) for space in in_spaces],
        out_specs=jax.tree.map(lambda _: pl.BlockSpec(memory_space=out_space), out_shape),
        scratch_shapes=list(scratch_shapes),
        compiler_params=pltpu.CompilerParams(vmem_limit_bytes=limit),
    )


def row_order(row_count):
    here = lax.axis_index("rep")
    turn = 2 * lax.rem(lax.axis_index("fsdp"), 2)
    return [lax.rem(here + by, row_count) for by in (0, 2, 1 + turn, 3 - turn)]


def split_kernel(row_count, halves, chosen, grads_ref, *refs):
    rows_at = row_order(row_count)
    outs, wide = refs[:-1], refs[-1]
    step = row_count * halves
    wide[...] = grads_ref[...].astype(F32)
    for n, out in zip(chosen, outs):
        for half in range(halves):
            part = wide[pl.ds(half * row_count + rows_at[n], out.shape[0], stride=step), :]
            out[:, half * LANES : (half + 1) * LANES] = part.astype(BF16)


def join_kernel(row_count, halves, *refs):
    rows_at = row_order(row_count)
    ins, (out_ref, near, wide, sems) = refs[:row_count], refs[row_count:]
    step = row_count * halves
    chunks = sems.shape[0]
    size = near.shape[0] // chunks
    copies = []
    for chunk in range(chunks):
        first, last = chunk * size, (chunk + 1) * size
        for n, rows in enumerate(ins):
            for half in range(halves):
                start = first + half * row_count + rows_at[n]
                part = rows[first // step : last // step, half * LANES : (half + 1) * LANES]
                wide[pl.ds(start, size // step, stride=step), :] = part.astype(F32)
        near[first:last, :] = wide[first:last, :].astype(BF16)
        span = pl.ds(first, size)
        copy = pltpu.make_async_copy(near.at[span], out_ref.at[span], sems.at[chunk])
        copy.start()
        copies.append(copy)
    for copy in copies:
        copy.wait()


def pick_kernel(halves, pick_ref, own_ref, two_ref, one_ref, three_ref, out_ref, wide):
    slots, owners = pick_ref.shape[:2]
    total = (
        own_ref[...].astype(F32)
        + one_ref[...].astype(F32)
        + two_ref[...].astype(F32)
        + three_ref[...].astype(F32)
    ).astype(BF16)
    for slot in range(slots):
        rows = jnp.dot(pick_ref[slot], total, preferred_element_type=F32)
        for half in range(halves):
            wide[pl.ds(half * slots + slot, owners, stride=halves * slots), :] = rows[
                :, half * LANES : (half + 1) * LANES
            ]
    out_ref[...] = wide[...].astype(BF16)


def place_kernel(halves, place_ref, got_ref, out_ref, wide):
    slots, _, owners = place_ref.shape
    wide[...] = got_ref[...].astype(F32)
    for half in range(halves):
        rows = 0.0
        for slot in range(slots):
            part = wide[pl.ds(half * slots + slot, owners, stride=halves * slots), :].astype(BF16)
            rows = rows + jnp.dot(place_ref[slot], part, preferred_element_type=F32)
        out_ref[:, half * LANES : (half + 1) * LANES] = rows.astype(BF16)


def update_kernel(
    halves, limits_ref, gather_ref, got_ref, lroot_ref, rroot_ref, moment_ref,
    grad_ref, out_ref, wide, wide_out,
):
    slots, size = grad_ref.shape[:2]
    owners = gather_ref.shape[1]
    step = slots * halves
    wide[...] = got_ref[...].astype(F32)
    row_ids = lax.broadcasted_iota(jnp.int32, (size, size), 0)
    col_ids = lax.broadcasted_iota(jnp.int32, (size, size), 1)
    for slot in range(slots):
        inside = (row_ids < limits_ref[0, slot]) & (col_ids < limits_ref[1, slot])
        parts = [
            wide[pl.ds(half * slots + slot, owners, stride=step), :].astype(BF16)
            for half in range(halves)
        ]
        block = jnp.dot(
            gather_ref[...], jnp.concatenate(parts, axis=1), preferred_element_type=F32
        ).astype(BF16)
        grad_wide = jnp.where(inside, block.astype(F32), 0.0)
        grad = grad_wide.astype(BF16)
        grad_ref[slot] = grad
        halfway = jnp.dot(lroot_ref[slot], grad, preferred_element_type=F32).astype(BF16)
        precond = jnp.dot(halfway, rroot_ref[slot], preferred_element_type=F32)
        precond = jnp.where(inside, precond, 0.0)
        moment = moment_decay * moment_ref[slot] + (1.0 - moment_decay) * grad_wide * grad_wide
        adam = grad_wide / (jnp.sqrt(moment) + adam_eps)
        adam_norm = jnp.sqrt(jnp.sum(adam * adam, axis=(0, 1), keepdims=True))
        pre_norm = jnp.sqrt(jnp.sum(precond * precond, axis=(0, 1), keepdims=True) + 1e-06)
        slot_update = (precond * (adam_norm / pre_norm)).astype(BF16)
        rows = lax.dot_general(
            gather_ref[...], slot_update, (((0,), (0,)), ((), ())), preferred_element_type=F32
        )
        for half in range(halves):
            wide_out[pl.ds(half * slots + slot, owners, stride=step), :] = rows[
                :, half * LANES : (half + 1) * LANES
            ]
    out_ref[...] = wide_out[...].astype(BF16)


def body(
    gradients,
    owned_blocks,
    rows_valid,
    cols_valid,
    left_factor,
    right_factor,
    left_root,
    right_root,
    second_moment,
):
    shards = lax.axis_size("fsdp")
    copies = lax.axis_size("rep")
    owners = shards * copies
    shard_index = lax.axis_index("fsdp")
    copy_index = lax.axis_index("rep")
    slab_count, row_count, col_count = gradients.shape[1:]
    size_b = left_factor.shape[-1]
    slot_count = owned_blocks.shape[2]
    block_total = slab_count * (col_count // size_b)
    halves = size_b // LANES
    tiles = col_count // LANES
    def crossed(operand, by):
        pairs = []
        for owner in range(shards):
            step = by if owner % 2 == 0 else -by
            pairs += [
                (owner * copies + i, owner * copies + (i + step) % copies) for i in range(copies)
            ]
        return lax.ppermute(operand, ("fsdp", "rep"), pairs)

    def everywhere(operand):
        return lax.all_to_all(operand, ("fsdp", "rep"), split_axis=0, concat_axis=0, tiled=True)

    rows_shape = jax.ShapeDtypeStruct((block_total, size_b), BF16)
    sent_shape = jax.ShapeDtypeStruct((owners * halves * slot_count, LANES), BF16)
    tile_rows = slab_count * tiles * row_count
    near_grads = pltpu.VMEM((tile_rows, LANES), BF16)
    wide_grads = pltpu.VMEM((tile_rows, LANES), F32)
    chunk_sems = pltpu.SemaphoreType.DMA((4,))
    wide_sent = pltpu.VMEM(sent_shape.shape, F32)

    by_tile = (
        gradients[0]
        .reshape(slab_count, row_count, tiles, LANES)
        .transpose(0, 2, 1, 3)
        .reshape(tile_rows, LANES)
    )
    (row_two,) = call(
        functools.partial(split_kernel, row_count, halves, (1,)),
        (rows_shape,),
        [wide_grads],
        [pltpu.VMEM],
    )(by_tile)
    by_tile, row_two = lax.optimization_barrier((by_tile, row_two))
    from_two = crossed(row_two, 2)
    row_zero, row_one, row_three = call(
        functools.partial(split_kernel, row_count, halves, (0, 2, 3)),
        (rows_shape,) * 3,
        [wide_grads],
        [pltpu.VMEM],
    )(by_tile)
    from_one = crossed(row_one, 1)
    from_three = crossed(row_three, -1)
    slot_ids = owned_blocks.reshape(owners, slot_count).T
    block_ids = jnp.arange(block_total, dtype=jnp.int32)
    pick = (slot_ids[:, :, None] == block_ids[None, None, :]).astype(BF16)
    place = (slot_ids[:, None, :] == block_ids[None, :, None]).astype(BF16)
    row = jnp.arange(size_b, dtype=jnp.int32)[:, None]
    source = jnp.arange(owners, dtype=jnp.int32)[None, :]
    gather = (
        (row // row_count == source // copies) & (row % row_count == source % row_count)
    ).astype(BF16)
    outgoing = call(
        functools.partial(pick_kernel, halves), sent_shape, [wide_sent], [pltpu.VMEM] * 5
    )(pick, row_zero, from_two, from_one, from_three)
    arrived = everywhere(outgoing)
    owned_here = owned_blocks[shard_index, copy_index]
    row_limit = jnp.take(rows_valid, owned_here, mode="fill", fill_value=0)
    col_limit = jnp.take(cols_valid, owned_here, mode="fill", fill_value=0)
    grad_block, parts_out = call(
        functools.partial(update_kernel, halves),
        (jax.ShapeDtypeStruct((slot_count, size_b, size_b), BF16), sent_shape),
        [wide_sent, wide_sent],
        [pltpu.SMEM] + [pltpu.VMEM] * 5,
    )(
        jnp.stack([row_limit, col_limit]),
        gather,
        arrived,
        left_root[0, 0],
        right_root[0, 0],
        second_moment[0, 0],
    )
    left_next = factor_decay * left_factor[0, 0] + (1.0 - factor_decay) * jnp.einsum(
        "kij,klj->kil", grad_block, grad_block, preferred_element_type=F32
    )
    right_next = factor_decay * right_factor[0, 0] + (1.0 - factor_decay) * jnp.einsum(
        "kji,kjl->kil", grad_block, grad_block, preferred_element_type=F32
    )
    returned = everywhere(parts_out)
    returned, left_next, right_next = lax.optimization_barrier((returned, left_next, right_next))
    placed = call(
        functools.partial(place_kernel, halves), rows_shape, [wide_sent], [pltpu.VMEM] * 2
    )(place, returned)
    row_two = crossed(placed, 2)
    row_one = crossed(placed, 1)
    row_three = crossed(placed, -1)
    joined = call(
        functools.partial(join_kernel, row_count, halves),
        jax.ShapeDtypeStruct((tile_rows, LANES), BF16),
        [near_grads, wide_grads, chunk_sems],
        [pltpu.VMEM] * row_count,
        out_space=pltpu.HBM,
    )(placed, row_two, row_three, row_one)
    update = (
        joined.reshape(slab_count, tiles, row_count, LANES)
        .transpose(0, 2, 1, 3)
        .reshape(slab_count, row_count, col_count)
    )
    return (update, left_next[None, None], right_next[None, None])


def solution(mesh):
    in_specs = (
        P("rep", None, "fsdp", None),
        P(),
        P(),
        P(),
        P("fsdp", "rep", None, None, None),
        P("fsdp", "rep", None, None, None),
        P("fsdp", "rep", None, None, None),
        P("fsdp", "rep", None, None, None),
        P("fsdp", "rep", None, None, None),
    )
    out_specs = (
        P(None, "fsdp", None),
        P("fsdp", "rep", None, None, None),
        P("fsdp", "rep", None, None, None),
    )
    return jax.shard_map(body, mesh=mesh, in_specs=in_specs, out_specs=out_specs, check_vma=False)
```

time: 280 us -> 121 us (0.43)
  waiting for transfers between devices: 135 us -> 55.7 us
  blocking collectives: 64.9 us -> 0 us
  local copies, waits for them, and re-layouts: 44.2 us -> 2.93 us
  starting transfers between devices: 11 us -> 49.9 us
  between operations: 14.2 us -> 0.84 us
  Pallas kernels: 0 us -> 7.44 us
  other arithmetic: 4.8 us -> 0.76 us
  matrix products: 5.1 us -> 2.13 us
    all_to_all x1 -> x0, blocking collectives: 64.9 us -> none  [body(): lax.all_to_all(outgoing, 'fsdp', split_axis=0, concat_axis=3, tiled=True)]
    all_gather x1 -> x0, waiting for transfers between devices: 49.3 us -> none  [body(): everyone = lax.all_gather(rows_split[None], 'rep', axis=0, tiled=True)]
    reduce_scatter x1 -> x0, waiting for transfers between devices: 38.4 us -> none  [body(): lax.psum_scatter(arrived[0].astype(jnp.float32).astype(jnp.bfloat16), 're...]
    scatter x2 -> x0, local copies, waits for them, and re-layouts: 28.1 us -> none  [body(): placed = jnp.zeros((block_total, row_count, size_b), jnp.bfloat16).at[slo...]
    ppermute x0 -> x6, starting transfers between devices: none -> 19.6 us  [crossed(): return lax.ppermute(operand, ('fsdp', 'rep'), pairs)]
    all_to_all x1 -> x2, starting transfers between devices: 10.9 us -> 30.2 us  [everywhere(): lax.all_to_all(operand, ('fsdp', 'rep'), split_axis=0, concat_axis=0, til...]
    ppermute x0 -> x6, waiting for transfers between devices: none -> 18.1 us  [crossed(): return lax.ppermute(operand, ('fsdp', 'rep'), pairs)]
    all_to_all x1 -> x2, waiting for transfers between devices: 47.5 us -> 37.6 us  [everywhere(): lax.all_to_all(operand, ('fsdp', 'rep'), split_axis=0, concat_axis=0, til...]
  transfers between devices with their start and end apart: 3 -> 8, of which waited for: 3 -> 6; matrix products, arithmetic and copies ran while one was open for 2% -> 4% of each run, Pallas kernels for 0% -> 0%
where the time goes in v2:
time: 121 us; the launch traced here: 120 us
  waiting for transfers between devices  55.7 us (46%)
  starting transfers between devices  49.9 us (41%)
  Pallas kernels  7.44 us (6%)
  local copies, waits for them, and re-layouts  2.93 us (2%)
  matrix products  2.13 us (2%)
    all_to_all x2, waiting for transfers between devices, everywhere(): lax.all_to_all(operand, ('fsdp', 'rep'), split_axis=0, concat_axis=0, til...  37.6 us
    all_to_all x2, starting transfers between devices, everywhere(): lax.all_to_all(operand, ('fsdp', 'rep'), split_axis=0, concat_axis=0, til...  30.2 us
    ppermute x6, starting transfers between devices, crossed(): return lax.ppermute(operand, ('fsdp', 'rep'), pairs)  19.6 us
    ppermute x6, waiting for transfers between devices, crossed(): return lax.ppermute(operand, ('fsdp', 'rep'), pairs)  18.1 us
    pallas_call x1, Pallas kernels, body(): call(functools.partial(update_kernel, halves), (jax.ShapeDtypeStruct((slo...  3.19 us
  transfers between devices with their start and end apart: 8, of which 6 were waited for; matrix products, arithmetic and copies ran while one was open for 4% of the time, Pallas kernels for 0%

profile of v2, /device:TPU:6, one launch (start us, length us, event | category | flops | bytes accessed | tf_op | source)
XLA Modules:
  0.0 119.6 jit_solution(14822430908707343958)
XLA Ops:
  0.7 1.2 %copy-done.1 = bf16[1,16,4,8192]{3,2,1,0:T(4,128)(2,1)S(1)} copy-done((bf16[1,16,4,8192]{3,2,1,0:T(4,128)(2,1)S(1)}, bf16[1,16,4,8192]{3,2,1,0:T(4,128)(2,1)}, u32[]{:S(2)}) %copy-start.1) | copy-done | bytes 1048600
  2.2 0.5 shard_map.113
  2.7 3.5 %collective-permute-start.1 = (bf16[512,256]{1,0:T(8,128)(2,1)S(1)}, bf16[512,256]{1,0:T(8,128)(2,1)S(1)}, u32[]{:S(2)}, u32[]{:S(2)}) collective-permute-start(bf16[512,256]{1,0:T(8,128)(2,1)S(1)} %get-tuple-element.17), channel_id=1, source_target_pairs={{0,1},{1,2},{2,3},{3,4},{4,5},{5,6},{6,7},{7,0},{8,15},{9,8},{10,9... | collective-permute-start | bytes 786440 | tf_op jit(solution)/shard_map/ppermute | solution.py:166
  6.2 3.8 %collective-permute-start.2 = (bf16[512,256]{1,0:T(8,128)(2,1)S(1)}, bf16[512,256]{1,0:T(8,128)(2,1)S(1)}, u32[]{:S(2)}, u32[]{:S(2)}) collective-permute-start(bf16[512,256]{1,0:T(8,128)(2,1)S(1)} %get-tuple-element.18), channel_id=1, source_target_pairs={{0,7},{1,0},{2,1},{3,2},{4,3},{5,4},{6,5},{7,6},{8,9},{9,10},{10,1... | collective-permute-start | bytes 786440 | tf_op jit(solution)/shard_map/ppermute | solution.py:166
  10.0 3.0 %collective-permute-start = (bf16[512,256]{1,0:T(8,128)(2,1)S(1)}, bf16[512,256]{1,0:T(8,128)(2,1)S(1)}, u32[]{:S(2)}, u32[]{:S(2)}) collective-permute-start(bf16[512,256]{1,0:T(8,128)(2,1)S(1)} %shard_map.112), channel_id=1, source_target_pairs={{0,2},{1,3},{2,4},{3,5},{4,6},{5,7},{6,0},{7,1},{8,14},{9,15},{10,... | collective-permute-start | bytes 786440 | tf_op jit(solution)/shard_map/ppermute | solution.py:166
  13.5 0.6 fusion.1
  14.5 8.8 %collective-permute-done.two_ref = bf16[512,256]{1,0:T(8,128)(2,1)S(1)} collective-permute-done((bf16[512,256]{1,0:T(8,128)(2,1)S(1)}, bf16[512,256]{1,0:T(8,128)(2,1)S(1)}, u32[]{:S(2)}, u32[]{:S(2)}) %collective-permute-start) | collective-permute-done | bytes 262176 | tf_op jit(solution)/shard_map/ppermute | solution.py:166
  23.2 1.3 %shard_map.114 = bf16[2048,128]{1,0:T(8,128)(2,1)} custom-call(bf16[2,512,512]{2,1,0:T(8,128)(2,1)S(1)} %get-tuple-element.24.pick_ref, bf16[512,256]{1,0:T(8,128)(2,1)S(1)} %get-tuple-element.15.own_ref, bf16[512,256]{1,0:T(8,128)(2,1)S(1)} %collective-permute-done.two_ref, bf16[512,256]{1,0:T(8,128)(2,1)S(1)} %collective-permute-done.1.one_ref, ...), custom_call_target="tpu_custom_call" | custom-call | tf_op jit(solution)/shard_map/pallas_call | solution.py:210
  24.6 19.4 %all-to-all-start = ((bf16[512,4,128]{2,1,0:T(4,128)(2,1)}), bf16[512,4,128]{2,1,0:T(4,128)(2,1)S(1)}, u32[]{:S(2)}, u32[]{:S(2)}) async-start(bf16[512,4,128]{2,1,0:T(4,128)(2,1)} %bitcast.8), calls=%async_computation | async-start | bytes 1048576 | tf_op jit(solution)/shard_map/all_to_all | solution.py:169
  44.0 0.6 gather_fusion
  44.7 0.6 gather_fusion.1
  45.5 19.1 %all-to-all-done = bf16[512,4,128]{2,1,0:T(4,128)(2,1)S(1)} async-done(((bf16[512,4,128]{2,1,0:T(4,128)(2,1)}), bf16[512,4,128]{2,1,0:T(4,128)(2,1)S(1)}, u32[]{:S(2)}, u32[]{:S(2)}) %all-to-all-start) | async-done | bytes 524320 | tf_op jit(solution)/shard_map/all_to_all | solution.py:169
  64.6 3.2 %shard_map.115 = (bf16[2,256,256]{2,1,0:T(8,128)(2,1)S(1)}, bf16[2048,128]{1,0:T(8,128)(2,1)}) custom-call(s32[2,2]{1,0:T(2,128)S(1)} %pad_add_fusion.limits_ref, bf16[256,512]{1,0:T(8,128)(2,1)S(1)} %and_convert_fusion.gather_ref, bf16[2048,128]{1,0:T(8,128)(2,1)S(1)} %bitcast.36, bf16[2,256,256]{2,1,0:T(8,128)(2,1)S(1)} %bitcast.39, ...), custom_call_target="tpu_custom_call" | custom-call | tf_op jit(solution)/shard_map/pallas_call | solution.py:217
  67.8 10.8 %all-to-all-start.1 = ((bf16[512,4,128]{2,1,0:T(4,128)(2,1)}), bf16[512,4,128]{2,1,0:T(4,128)(2,1)S(1)}, u32[]{:S(2)}, u32[]{:S(2)}) async-start(bf16[512,4,128]{2,1,0:T(4,128)(2,1)} %bitcast.13), calls=%async_computation.1 | async-start | bytes 1048576 | tf_op jit(solution)/shard_map/all_to_all | solution.py:169
  78.6 1.1 fusion.2
  79.7 1.1 fusion.3
  80.8 18.5 %all-to-all-done.1 = bf16[512,4,128]{2,1,0:T(4,128)(2,1)S(1)} async-done(((bf16[512,4,128]{2,1,0:T(4,128)(2,1)}), bf16[512,4,128]{2,1,0:T(4,128)(2,1)S(1)}, u32[]{:S(2)}, u32[]{:S(2)}) %all-to-all-start.1) | async-done | bytes 524320 | tf_op jit(solution)/shard_map/all_to_all | solution.py:169
  99.3 0.7 shard_map.116.refs_0_
  100.0 3.0 %collective-permute-start.3 = (bf16[512,256]{1,0:T(8,128)(2,1)S(1)}, bf16[512,256]{1,0:T(8,128)(2,1)S(1)}, u32[]{:S(2)}, u32[]{:S(2)}) collective-permute-start(bf16[512,256]{1,0:T(8,128)(2,1)S(1)} %shard_map.116.refs_0_), channel_id=1, source_target_pairs={{0,2},{1,3},{2,4},{3,5},{4,6},{5,7},{6,0},{7,1},{8,14},{9,15},{10,... | collective-permute-start | bytes 786440 | tf_op jit(solution)/shard_map/ppermute | solution.py:166
  103.0 4.4 %collective-permute-start.4 = (bf16[512,256]{1,0:T(8,128)(2,1)S(1)}, bf16[512,256]{1,0:T(8,128)(2,1)S(1)}, u32[]{:S(2)}, u32[]{:S(2)}) collective-permute-start(bf16[512,256]{1,0:T(8,128)(2,1)S(1)} %shard_map.116.refs_0_), channel_id=1, source_target_pairs={{0,7},{1,0},{2,1},{3,2},{4,3},{5,4},{6,5},{7,6},{8,9},{9,10},{10,1... | collective-permute-start | bytes 786440 | tf_op jit(solution)/shard_map/ppermute | solution.py:166
  107.4 1.9 %collective-permute-start.5 = (bf16[512,256]{1,0:T(8,128)(2,1)S(1)}, bf16[512,256]{1,0:T(8,128)(2,1)S(1)}, u32[]{:S(2)}, u32[]{:S(2)}) collective-permute-start(bf16[512,256]{1,0:T(8,128)(2,1)S(1)} %shard_map.116.refs_0_), channel_id=1, source_target_pairs={{0,1},{1,2},{2,3},{3,4},{4,5},{5,6},{6,7},{7,0},{8,15},{9,8},{10,9... | collective-permute-start | bytes 786440 | tf_op jit(solution)/shard_map/ppermute | solution.py:166
  109.3 6.3 %collective-permute-done.3.refs_1_ = bf16[512,256]{1,0:T(8,128)(2,1)S(1)} collective-permute-done((bf16[512,256]{1,0:T(8,128)(2,1)S(1)}, bf16[512,256]{1,0:T(8,128)(2,1)S(1)}, u32[]{:S(2)}, u32[]{:S(2)}) %collective-permute-start.3) | collective-permute-done | bytes 262176 | tf_op jit(solution)/shard_map/ppermute | solution.py:166
  115.7 2.6 %collective-permute-done.5.refs_3_ = bf16[512,256]{1,0:T(8,128)(2,1)S(1)} collective-permute-done((bf16[512,256]{1,0:T(8,128)(2,1)S(1)}, bf16[512,256]{1,0:T(8,128)(2,1)S(1)}, u32[]{:S(2)}, u32[]{:S(2)}) %collective-permute-start.5) | collective-permute-done | bytes 262176 | tf_op jit(solution)/shard_map/ppermute | solution.py:166
  118.3 1.4 %shard_map.117 = bf16[4096,128]{1,0:T(8,128)(2,1)} custom-call(bf16[512,256]{1,0:T(8,128)(2,1)S(1)} %shard_map.116.refs_0_, bf16[512,256]{1,0:T(8,128)(2,1)S(1)} %collective-permute-done.3.refs_1_, bf16[512,256]{1,0:T(8,128)(2,1)S(1)} %collective-permute-done.4.refs_2_, bf16[512,256]{1,0:T(8,128)(2,1)S(1)} %collective-permute-done.5.refs_3_), custom_call_target="tpu_custom_call" | custom-call | tf_op jit(solution)/shard_map/pallas_call | solution.py:244
  (31 shorter events, 1.3 us)
Async XLA Ops:
  0.6 43.4 %copy-start = (s32[512]{0:T(512)S(1)}, s32[512]{0:T(512)}, u32[]{:S(2)}) copy-start(s32[512]{0:T(512)} %param.13) | copy-start | bytes 6148
  0.6 1.2 %copy-start.1 = (bf16[1,16,4,8192]{3,2,1,0:T(4,128)(2,1)S(1)}, bf16[1,16,4,8192]{3,2,1,0:T(4,128)(2,1)}, u32[]{:S(2)}) copy-start(bf16[1,16,4,8192]{3,2,1,0:T(4,128)(2,1)} %param.11) | copy-start | bytes 3145732
  1.9 11.2 %copy-start.8 = (s32[64,8,2]{0,2,1:T(2,128)S(1)}, s32[64,8,2]{0,2,1:T(2,128)}, u32[]{:S(2)}) copy-start(s32[64,8,2]{0,2,1:T(2,128)} %param.12) | copy-start | bytes 12292
  2.7 11.4 %collective-permute-start.1 = (bf16[512,256]{1,0:T(8,128)(2,1)S(1)}, bf16[512,256]{1,0:T(8,128)(2,1)S(1)}, u32[]{:S(2)}, u32[]{:S(2)}) collective-permute-start(bf16[512,256]{1,0:T(8,128)(2,1)S(1)} %get-tuple-element.17), channel_id=1, source_target_pairs={{0,1},{1,2},{2,3},{3,4},{4,5},{5,6},{6,7},{7,0},{8,15},{9,8},{10,9... | collective-permute-start | bytes 786440 | tf_op jit(solution)/shard_map/ppermute | solution.py:166
  6.2 8.3 %collective-permute-start.2 = (bf16[512,256]{1,0:T(8,128)(2,1)S(1)}, bf16[512,256]{1,0:T(8,128)(2,1)S(1)}, u32[]{:S(2)}, u32[]{:S(2)}) collective-permute-start(bf16[512,256]{1,0:T(8,128)(2,1)S(1)} %get-tuple-element.18), channel_id=1, source_target_pairs={{0,7},{1,0},{2,1},{3,2},{4,3},{5,4},{6,5},{7,6},{8,9},{9,10},{10,1... | collective-permute-start | bytes 786440 | tf_op jit(solution)/shard_map/ppermute | solution.py:166
  10.0 13.2 %collective-permute-start = (bf16[512,256]{1,0:T(8,128)(2,1)S(1)}, bf16[512,256]{1,0:T(8,128)(2,1)S(1)}, u32[]{:S(2)}, u32[]{:S(2)}) collective-permute-start(bf16[512,256]{1,0:T(8,128)(2,1)S(1)} %shard_map.112), channel_id=1, source_target_pairs={{0,2},{1,3},{2,4},{3,5},{4,6},{5,7},{6,0},{7,1},{8,14},{9,15},{10,... | collective-permute-start | bytes 786440 | tf_op jit(solution)/shard_map/ppermute | solution.py:166
  24.6 20.1 %copy-start.5 = (s32[512]{0:T(512)S(1)}, s32[512]{0:T(512)}, u32[]{:S(2)}) copy-start(s32[512]{0:T(512)} %param.14) | copy-start | bytes 6148
  24.6 40.0 %copy-start.2 = (f32[1,1,2,256,256]{4,3,2,1,0:T(8,128)S(1)}, f32[1,1,2,256,256]{4,3,2,1,0:T(8,128)}, u32[]{:S(2)}) copy-start(f32[1,1,2,256,256]{4,3,2,1,0:T(8,128)} %param.19) | copy-start | bytes 1572868
  24.6 40.0 %copy-start.3 = (bf16[1,1,2,256,256]{4,3,2,1,0:T(8,128)(2,1)S(1)}, bf16[1,1,2,256,256]{4,3,2,1,0:T(8,128)(2,1)}, u32[]{:S(2)}) copy-start(bf16[1,1,2,256,256]{4,3,2,1,0:T(8,128)(2,1)} %param.17) | copy-start | bytes 786436
  24.6 40.0 %copy-start.4 = (bf16[1,1,2,256,256]{4,3,2,1,0:T(8,128)(2,1)S(1)}, bf16[1,1,2,256,256]{4,3,2,1,0:T(8,128)(2,1)}, u32[]{:S(2)}) copy-start(bf16[1,1,2,256,256]{4,3,2,1,0:T(8,128)(2,1)} %param.18) | copy-start | bytes 786436
  24.6 40.0 %all-to-all-start = ((bf16[512,4,128]{2,1,0:T(4,128)(2,1)}), bf16[512,4,128]{2,1,0:T(4,128)(2,1)S(1)}, u32[]{:S(2)}, u32[]{:S(2)}) async-start(bf16[512,4,128]{2,1,0:T(4,128)(2,1)} %bitcast.8), calls=%async_computation | async-start | bytes 1048576 | tf_op jit(solution)/shard_map/all_to_all | solution.py:169
  67.8 10.8 %copy-start.6 = (f32[1,1,2,256,256]{4,3,2,1,0:T(8,128)S(1)}, f32[1,1,2,256,256]{4,3,2,1,0:T(8,128)}, u32[]{:S(2)}) copy-start(f32[1,1,2,256,256]{4,3,2,1,0:T(8,128)} %param.16) | copy-start | bytes 1572868
  67.8 31.5 %all-to-all-start.1 = ((bf16[512,4,128]{2,1,0:T(4,128)(2,1)}), bf16[512,4,128]{2,1,0:T(4,128)(2,1)S(1)}, u32[]{:S(2)}, u32[]{:S(2)}) async-start(bf16[512,4,128]{2,1,0:T(4,128)(2,1)} %bitcast.13), calls=%async_computation.1 | async-start | bytes 1048576 | tf_op jit(solution)/shard_map/all_to_all | solution.py:169
  78.6 1.1 copy-start.7
  100.0 15.6 %collective-permute-start.3 = (bf16[512,256]{1,0:T(8,128)(2,1)S(1)}, bf16[512,256]{1,0:T(8,128)(2,1)S(1)}, u32[]{:S(2)}, u32[]{:S(2)}) collective-permute-start(bf16[512,256]{1,0:T(8,128)(2,1)S(1)} %shard_map.116.refs_0_), channel_id=1, source_target_pairs={{0,2},{1,3},{2,4},{3,5},{4,6},{5,7},{6,0},{7,1},{8,14},{9,15},{10,... | collective-permute-start | bytes 786440 | tf_op jit(solution)/shard_map/ppermute | solution.py:166
  103.0 12.6 %collective-permute-start.4 = (bf16[512,256]{1,0:T(8,128)(2,1)S(1)}, bf16[512,256]{1,0:T(8,128)(2,1)S(1)}, u32[]{:S(2)}, u32[]{:S(2)}) collective-permute-start(bf16[512,256]{1,0:T(8,128)(2,1)S(1)} %shard_map.116.refs_0_), channel_id=1, source_target_pairs={{0,7},{1,0},{2,1},{3,2},{4,3},{5,4},{6,5},{7,6},{8,9},{9,10},{10,1... | collective-permute-start | bytes 786440 | tf_op jit(solution)/shard_map/ppermute | solution.py:166
  107.4 10.8 %collective-permute-start.5 = (bf16[512,256]{1,0:T(8,128)(2,1)S(1)}, bf16[512,256]{1,0:T(8,128)(2,1)S(1)}, u32[]{:S(2)}, u32[]{:S(2)}) collective-permute-start(bf16[512,256]{1,0:T(8,128)(2,1)S(1)} %shard_map.116.refs_0_), channel_id=1, source_target_pairs={{0,1},{1,2},{2,3},{3,4},{4,5},{5,6},{6,7},{7,0},{8,15},{9,8},{10,9... | collective-permute-start | bytes 786440 | tf_op jit(solution)/shard_map/ppermute | solution.py:166

commit v3 on v2

--- a/solution.py
+++ b/solution.py
@@ -32,12 +32,12 @@
     return [lax.rem(here + by, row_count) for by in (0, 2, 1 + turn, 3 - turn)]
 
 
-def split_kernel(row_count, halves, chosen, grads_ref, *refs):
+def split_kernel(row_count, halves, grads_ref, *refs):
     rows_at = row_order(row_count)
     outs, wide = refs[:-1], refs[-1]
     step = row_count * halves
     wide[...] = grads_ref[...].astype(F32)
-    for n, out in zip(chosen, outs):
+    for n, out in enumerate(outs):
         for half in range(halves):
             part = wide[pl.ds(half * row_count + rows_at[n], out.shape[0], stride=step), :]
             out[:, half * LANES : (half + 1) * LANES] = part.astype(BF16)
@@ -86,12 +86,16 @@
 def place_kernel(halves, place_ref, got_ref, out_ref, wide):
     slots, _, owners = place_ref.shape
     wide[...] = got_ref[...].astype(F32)
-    for half in range(halves):
-        rows = 0.0
-        for slot in range(slots):
-            part = wide[pl.ds(half * slots + slot, owners, stride=halves * slots), :].astype(BF16)
-            rows = rows + jnp.dot(place_ref[slot], part, preferred_element_type=F32)
-        out_ref[:, half * LANES : (half + 1) * LANES] = rows.astype(BF16)
+    rows = 0.0
+    for slot in range(slots):
+        parts = [
+            wide[pl.ds(half * slots + slot, owners, stride=halves * slots), :].astype(BF16)
+            for half in range(halves)
+        ]
+        rows = rows + jnp.dot(
+            place_ref[slot], jnp.concatenate(parts, axis=1), preferred_element_type=F32
+        )
+    out_ref[...] = rows.astype(BF16)
 
 
 def update_kernel(
@@ -101,35 +105,53 @@
     slots, size = grad_ref.shape[:2]
     owners = gather_ref.shape[1]
     step = slots * halves
+    every = range(slots)
     wide[...] = got_ref[...].astype(F32)
     row_ids = lax.broadcasted_iota(jnp.int32, (size, size), 0)
     col_ids = lax.broadcasted_iota(jnp.int32, (size, size), 1)
-    for slot in range(slots):
-        inside = (row_ids < limits_ref[0, slot]) & (col_ids < limits_ref[1, slot])
-        parts = [
-            wide[pl.ds(half * slots + slot, owners, stride=step), :].astype(BF16)
-            for half in range(halves)
-        ]
-        block = jnp.dot(
-            gather_ref[...], jnp.concatenate(parts, axis=1), preferred_element_type=F32
-        ).astype(BF16)
-        grad_wide = jnp.where(inside, block.astype(F32), 0.0)
-        grad = grad_wide.astype(BF16)
-        grad_ref[slot] = grad
-        halfway = jnp.dot(lroot_ref[slot], grad, preferred_element_type=F32).astype(BF16)
-        precond = jnp.dot(halfway, rroot_ref[slot], preferred_element_type=F32)
-        precond = jnp.where(inside, precond, 0.0)
+    parts = [
+        wide[pl.ds(half * slots + slot, owners, stride=step), :].astype(BF16)
+        for slot in every
+        for half in range(halves)
+    ]
+    blocks = jnp.dot(
+        gather_ref[...], jnp.concatenate(parts, axis=1), preferred_element_type=F32
+    ).astype(BF16)
+    inside, wides, grads = [], [], []
+    for slot in every:
+        inside.append((row_ids < limits_ref[0, slot]) & (col_ids < limits_ref[1, slot]))
+        block = blocks[:, slot * size : (slot + 1) * size].astype(F32)
+        wides.append(jnp.where(inside[slot], block, 0.0))
+        grads.append(wides[slot].astype(BF16))
+        grad_ref[slot] = grads[slot]
+    halfway = [
+        jnp.dot(lroot_ref[slot], grads[slot], preferred_element_type=F32).astype(BF16)
+        for slot in every
+    ]
+    preconds = [
+        jnp.where(
+            inside[slot], jnp.dot(halfway[slot], rroot_ref[slot], preferred_element_type=F32), 0.0
+        )
+        for slot in every
+    ]
+    updates = []
+    for slot, (grad_wide, precond) in enumerate(zip(wides, preconds)):
         moment = moment_decay * moment_ref[slot] + (1.0 - moment_decay) * grad_wide * grad_wide
         adam = grad_wide / (jnp.sqrt(moment) + adam_eps)
         adam_norm = jnp.sqrt(jnp.sum(adam * adam, axis=(0, 1), keepdims=True))
         pre_norm = jnp.sqrt(jnp.sum(precond * precond, axis=(0, 1), keepdims=True) + 1e-06)
-        slot_update = (precond * (adam_norm / pre_norm)).astype(BF16)
-        rows = lax.dot_general(
-            gather_ref[...], slot_update, (((0,), (0,)), ((), ())), preferred_element_type=F32
-        )
+        updates.append((precond * (adam_norm / pre_norm)).astype(BF16))
+    rows = lax.dot_general(
+        gather_ref[...],
+        jnp.concatenate(updates, axis=1),
+        (((0,), (0,)), ((), ())),
+        preferred_element_type=F32,
+    )
+    for slot in every:
         for half in range(halves):
+            first = slot * size + half * LANES
             wide_out[pl.ds(half * slots + slot, owners, stride=step), :] = rows[
-                :, half * LANES : (half + 1) * LANES
+                :, first : first + LANES
             ]
     out_ref[...] = wide_out[...].astype(BF16)
 
@@ -182,20 +204,13 @@
         .transpose(0, 2, 1, 3)
         .reshape(tile_rows, LANES)
     )
-    (row_two,) = call(
-        functools.partial(split_kernel, row_count, halves, (1,)),
-        (rows_shape,),
+    row_zero, row_two, row_one, row_three = call(
+        functools.partial(split_kernel, row_count, halves),
+        (rows_shape,) * row_count,
         [wide_grads],
         [pltpu.VMEM],
     )(by_tile)
-    by_tile, row_two = lax.optimization_barrier((by_tile, row_two))
     from_two = crossed(row_two, 2)
-    row_zero, row_one, row_three = call(
-        functools.partial(split_kernel, row_count, halves, (0, 2, 3)),
-        (rows_shape,) * 3,
-        [wide_grads],
-        [pltpu.VMEM],
-    )(by_tile)
     from_one = crossed(row_one, 1)
     from_three = crossed(row_three, -1)
     slot_ids = owned_blocks.reshape(owners, slot_count).T
@@ -210,37 +225,39 @@
     outgoing = call(
         functools.partial(pick_kernel, halves), sent_shape, [wide_sent], [pltpu.VMEM] * 5
     )(pick, row_zero, from_two, from_one, from_three)
-    arrived = everywhere(outgoing)
     owned_here = owned_blocks[shard_index, copy_index]
     row_limit = jnp.take(rows_valid, owned_here, mode="fill", fill_value=0)
     col_limit = jnp.take(cols_valid, owned_here, mode="fill", fill_value=0)
+    limits = jnp.stack([row_limit, col_limit])
+    outgoing, limits, gather = lax.optimization_barrier((outgoing, limits, gather))
+    arrived = everywhere(outgoing)
     grad_block, parts_out = call(
         functools.partial(update_kernel, halves),
         (jax.ShapeDtypeStruct((slot_count, size_b, size_b), BF16), sent_shape),
         [wide_sent, wide_sent],
         [pltpu.SMEM] + [pltpu.VMEM] * 5,
     )(
-        jnp.stack([row_limit, col_limit]),
+        limits,
         gather,
         arrived,
         left_root[0, 0],
         right_root[0, 0],
         second_moment[0, 0],
     )
-    left_next = factor_decay * left_factor[0, 0] + (1.0 - factor_decay) * jnp.einsum(
-        "kij,klj->kil", grad_block, grad_block, preferred_element_type=F32
-    )
-    right_next = factor_decay * right_factor[0, 0] + (1.0 - factor_decay) * jnp.einsum(
-        "kji,kjl->kil", grad_block, grad_block, preferred_element_type=F32
-    )
     returned = everywhere(parts_out)
-    returned, left_next, right_next = lax.optimization_barrier((returned, left_next, right_next))
     placed = call(
         functools.partial(place_kernel, halves), rows_shape, [wide_sent], [pltpu.VMEM] * 2
     )(place, returned)
     row_two = crossed(placed, 2)
     row_one = crossed(placed, 1)
     row_three = crossed(placed, -1)
+    row_two, grad_block = lax.optimization_barrier((row_two, grad_block))
+    left_next = factor_decay * left_factor[0, 0] + (1.0 - factor_decay) * jnp.einsum(
+        "kij,klj->kil", grad_block, grad_block, preferred_element_type=F32
+    )
+    right_next = factor_decay * right_factor[0, 0] + (1.0 - factor_decay) * jnp.einsum(
+        "kji,kjl->kil", grad_block, grad_block, preferred_element_type=F32
+    )
     joined = call(
         functools.partial(join_kernel, row_count, halves),
         jax.ShapeDtypeStruct((tile_rows, LANES), BF16),

time: 121 us -> 118 us (0.975)
  blocking collectives: 0 us -> 73.5 us
  waiting for transfers between devices: 55.7 us -> 10.4 us
  starting transfers between devices: 49.9 us -> 21 us
  Pallas kernels: 7.44 us -> 5.05 us
    all_to_all x0 -> x2, blocking collectives: none -> 73.5 us  [everywhere(): lax.all_to_all(operand, ('fsdp', 'rep'), split_axis=0, concat_axis=0, til...]
    all_to_all x2 -> x0, waiting for transfers between devices: 37.6 us -> none  [everywhere(): lax.all_to_all(operand, ('fsdp', 'rep'), split_axis=0, concat_axis=0, til...]
    all_to_all x2 -> x0, starting transfers between devices: 30.2 us -> none  [everywhere(): lax.all_to_all(operand, ('fsdp', 'rep'), split_axis=0, concat_axis=0, til...]
    ppermute x6, waiting for transfers between devices: 18.1 us -> 10.4 us  [crossed(): return lax.ppermute(operand, ('fsdp', 'rep'), pairs)]
    ppermute x6, starting transfers between devices: 19.6 us -> 21 us  [crossed(): return lax.ppermute(operand, ('fsdp', 'rep'), pairs)]
  transfers between devices with their start and end apart: 8 -> 6, of which waited for: 6 -> 3; matrix products, arithmetic and copies ran while one was open for 4% -> 4% of each run, Pallas kernels for 0% -> 0%
where the time goes in v3:
time: 118 us; the launch traced here: 117 us
  blocking collectives  73.5 us (62%)
  starting transfers between devices  21 us (18%)
  waiting for transfers between devices  10.4 us (9%)
  Pallas kernels  5.05 us (4%)
  local copies, waits for them, and re-layouts  2.93 us (2%)
  matrix products  2.13 us (2%)
    all_to_all x2, blocking collectives, everywhere(): lax.all_to_all(operand, ('fsdp', 'rep'), split_axis=0, concat_axis=0, til...  73.5 us
    ppermute x6, starting transfers between devices, crossed(): return lax.ppermute(operand, ('fsdp', 'rep'), pairs)  21 us
    ppermute x6, waiting for transfers between devices, crossed(): return lax.ppermute(operand, ('fsdp', 'rep'), pairs)  10.4 us
  transfers between devices with their start and end apart: 6, of which 3 were waited for; matrix products, arithmetic and copies ran while one was open for 4% of the time, Pallas kernels for 0%

profile of v3, /device:TPU:6, one launch (start us, length us, event | category | flops | bytes accessed | tf_op | source)
XLA Modules:
  0.0 116.6 jit_solution(5179754221537388302)
XLA Ops:
  0.7 1.2 %copy-done.1 = bf16[1,16,4,8192]{3,2,1,0:T(4,128)(2,1)S(1)} copy-done((bf16[1,16,4,8192]{3,2,1,0:T(4,128)(2,1)S(1)}, bf16[1,16,4,8192]{3,2,1,0:T(4,128)(2,1)}, u32[]{:S(2)}) %copy-start.1) | copy-done | bytes 1048600
  1.9 0.6 shard_map.112
  2.5 4.5 %collective-permute-start = (bf16[512,256]{1,0:T(8,128)(2,1)S(1)}, bf16[512,256]{1,0:T(8,128)(2,1)S(1)}, u32[]{:S(2)}, u32[]{:S(2)}) collective-permute-start(bf16[512,256]{1,0:T(8,128)(2,1)S(1)} %get-tuple-element.16), channel_id=1, source_target_pairs={{0,2},{1,3},{2,4},{3,5},{4,6},{5,7},{6,0},{7,1},{8,14},{9,15},{10,... | collective-permute-start | bytes 786440 | tf_op jit(solution)/shard_map/ppermute | solution.py:188
  7.0 3.5 %collective-permute-start.1 = (bf16[512,256]{1,0:T(8,128)(2,1)S(1)}, bf16[512,256]{1,0:T(8,128)(2,1)S(1)}, u32[]{:S(2)}, u32[]{:S(2)}) collective-permute-start(bf16[512,256]{1,0:T(8,128)(2,1)S(1)} %get-tuple-element.17), channel_id=1, source_target_pairs={{0,1},{1,2},{2,3},{3,4},{4,5},{5,6},{6,7},{7,0},{8,15},{9,8},{10,9... | collective-permute-start | bytes 786440 | tf_op jit(solution)/shard_map/ppermute | solution.py:188
  10.5 3.6 %collective-permute-start.2 = (bf16[512,256]{1,0:T(8,128)(2,1)S(1)}, bf16[512,256]{1,0:T(8,128)(2,1)S(1)}, u32[]{:S(2)}, u32[]{:S(2)}) collective-permute-start(bf16[512,256]{1,0:T(8,128)(2,1)S(1)} %get-tuple-element.18), channel_id=1, source_target_pairs={{0,7},{1,0},{2,1},{3,2},{4,3},{5,4},{6,5},{7,6},{8,9},{9,10},{10,1... | collective-permute-start | bytes 786440 | tf_op jit(solution)/shard_map/ppermute | solution.py:188
  14.3 0.2 dynamic-slice_reduce_fusion
  14.6 0.6 gather_fusion
  15.2 0.6 gather_fusion.1
  15.9 0.1 and_convert_fusion.gather_ref
  16.0 0.6 fusion.1
  16.6 3.7 %collective-permute-done.1.one_ref = bf16[512,256]{1,0:T(8,128)(2,1)S(1)} collective-permute-done((bf16[512,256]{1,0:T(8,128)(2,1)S(1)}, bf16[512,256]{1,0:T(8,128)(2,1)S(1)}, u32[]{:S(2)}, u32[]{:S(2)}) %collective-permute-start.1) | collective-permute-done | bytes 262176 | tf_op jit(solution)/shard_map/ppermute | solution.py:188
  20.3 0.5 shard_map.113
  20.8 41.8 %all_to_all.22 = bf16[512,4,128]{2,1,0:T(4,128)(2,1)S(1)} all-to-all(bf16[512,4,128]{2,1,0:T(4,128)(2,1)S(1)} %bitcast.36), channel_id=1, replica_groups=mesh['fsdp'=64,'rep'=8] {'fsdp','rep'}, dimensions={0} | all-to-all | bytes 1048576 | tf_op jit(solution)/shard_map/all_to_all | solution.py:191
  62.7 2.0 %shard_map.114 = (bf16[2,256,256]{2,1,0:T(8,128)(2,1)S(1)}, bf16[2048,128]{1,0:T(8,128)(2,1)S(1)}) custom-call(s32[2,2]{1,0:T(2,128)S(1)} %pad_add_fusion.limits_ref, bf16[256,512]{1,0:T(8,128)(2,1)S(1)} %and_convert_fusion.gather_ref, bf16[2048,128]{1,0:T(8,128)(2,1)S(1)} %bitcast.37, bf16[2,256,256]{2,1,0:T(8,128)(2,1)S(1)} %bitcast.42, ...), custom_call_target="tpu_custom_call" | custom-call | tf_op jit(solution)/shard_map/pallas_call | solution.py:234
  64.7 31.7 %all_to_all.23 = bf16[512,4,128]{2,1,0:T(4,128)(2,1)S(1)} all-to-all(bf16[512,4,128]{2,1,0:T(4,128)(2,1)S(1)} %bitcast.41), channel_id=1, replica_groups=mesh['fsdp'=64,'rep'=8] {'fsdp','rep'}, dimensions={0} | all-to-all | bytes 1048576 | tf_op jit(solution)/shard_map/all_to_all | solution.py:191
  96.4 0.5 shard_map.115.refs_0_
  96.9 3.1 %collective-permute-start.3 = (bf16[512,256]{1,0:T(8,128)(2,1)S(1)}, bf16[512,256]{1,0:T(8,128)(2,1)S(1)}, u32[]{:S(2)}, u32[]{:S(2)}) collective-permute-start(bf16[512,256]{1,0:T(8,128)(2,1)S(1)} %shard_map.115.refs_0_), channel_id=1, source_target_pairs={{0,2},{1,3},{2,4},{3,5},{4,6},{5,7},{6,0},{7,1},{8,14},{9,15},{10,... | collective-permute-start | bytes 786440 | tf_op jit(solution)/shard_map/ppermute | solution.py:188
  100.0 4.4 %collective-permute-start.4 = (bf16[512,256]{1,0:T(8,128)(2,1)S(1)}, bf16[512,256]{1,0:T(8,128)(2,1)S(1)}, u32[]{:S(2)}, u32[]{:S(2)}) collective-permute-start(bf16[512,256]{1,0:T(8,128)(2,1)S(1)} %shard_map.115.refs_0_), channel_id=1, source_target_pairs={{0,7},{1,0},{2,1},{3,2},{4,3},{5,4},{6,5},{7,6},{8,9},{9,10},{10,1... | collective-permute-start | bytes 786440 | tf_op jit(solution)/shard_map/ppermute | solution.py:188
  104.4 1.9 %collective-permute-start.5 = (bf16[512,256]{1,0:T(8,128)(2,1)S(1)}, bf16[512,256]{1,0:T(8,128)(2,1)S(1)}, u32[]{:S(2)}, u32[]{:S(2)}) collective-permute-start(bf16[512,256]{1,0:T(8,128)(2,1)S(1)} %shard_map.115.refs_0_), channel_id=1, source_target_pairs={{0,1},{1,2},{2,3},{3,4},{4,5},{5,6},{6,7},{7,0},{8,15},{9,8},{10,9... | collective-permute-start | bytes 786440 | tf_op jit(solution)/shard_map/ppermute | solution.py:188
  106.3 6.3 %collective-permute-done.3.refs_1_ = bf16[512,256]{1,0:T(8,128)(2,1)S(1)} collective-permute-done((bf16[512,256]{1,0:T(8,128)(2,1)S(1)}, bf16[512,256]{1,0:T(8,128)(2,1)S(1)}, u32[]{:S(2)}, u32[]{:S(2)}) %collective-permute-start.3) | collective-permute-done | bytes 262176 | tf_op jit(solution)/shard_map/ppermute | solution.py:188
  112.6 1.1 fusion.3
  113.7 1.1 fusion.5
  114.8 0.5 collective-permute-done.5.refs_3_
  115.2 1.4 %shard_map.116 = bf16[4096,128]{1,0:T(8,128)(2,1)} custom-call(bf16[512,256]{1,0:T(8,128)(2,1)S(1)} %shard_map.115.refs_0_, bf16[512,256]{1,0:T(8,128)(2,1)S(1)} %collective-permute-done.3.refs_1_, bf16[512,256]{1,0:T(8,128)(2,1)S(1)} %collective-permute-done.4.refs_2_, bf16[512,256]{1,0:T(8,128)(2,1)S(1)} %collective-permute-done.5.refs_3_), custom_call_target="tpu_custom_call" | custom-call | tf_op jit(solution)/shard_map/pallas_call | solution.py:261
  (28 shorter events, 0.3 us)
Async XLA Ops:
  0.6 13.9 %copy-start = (s32[512]{0:T(512)S(1)}, s32[512]{0:T(512)}, u32[]{:S(2)}) copy-start(s32[512]{0:T(512)} %param.13) | copy-start | bytes 6148
  0.6 1.2 %copy-start.1 = (bf16[1,16,4,8192]{3,2,1,0:T(4,128)(2,1)S(1)}, bf16[1,16,4,8192]{3,2,1,0:T(4,128)(2,1)}, u32[]{:S(2)}) copy-start(bf16[1,16,4,8192]{3,2,1,0:T(4,128)(2,1)} %param.11) | copy-start | bytes 3145732
  1.9 12.2 %copy-start.8 = (s32[64,8,2]{0,2,1:T(2,128)S(1)}, s32[64,8,2]{0,2,1:T(2,128)}, u32[]{:S(2)}) copy-start(s32[64,8,2]{0,2,1:T(2,128)} %param.12) | copy-start | bytes 12292
  1.9 13.3 %copy-start.5 = (s32[512]{0:T(512)S(1)}, s32[512]{0:T(512)}, u32[]{:S(2)}) copy-start(s32[512]{0:T(512)} %param.14) | copy-start | bytes 6148
  2.5 14.1 %collective-permute-start = (bf16[512,256]{1,0:T(8,128)(2,1)S(1)}, bf16[512,256]{1,0:T(8,128)(2,1)S(1)}, u32[]{:S(2)}, u32[]{:S(2)}) collective-permute-start(bf16[512,256]{1,0:T(8,128)(2,1)S(1)} %get-tuple-element.16), channel_id=1, source_target_pairs={{0,2},{1,3},{2,4},{3,5},{4,6},{5,7},{6,0},{7,1},{8,14},{9,15},{10,... | collective-permute-start | bytes 786440 | tf_op jit(solution)/shard_map/ppermute | solution.py:188
  7.0 13.2 %collective-permute-start.1 = (bf16[512,256]{1,0:T(8,128)(2,1)S(1)}, bf16[512,256]{1,0:T(8,128)(2,1)S(1)}, u32[]{:S(2)}, u32[]{:S(2)}) collective-permute-start(bf16[512,256]{1,0:T(8,128)(2,1)S(1)} %get-tuple-element.17), channel_id=1, source_target_pairs={{0,1},{1,2},{2,3},{3,4},{4,5},{5,6},{6,7},{7,0},{8,15},{9,8},{10,9... | collective-permute-start | bytes 786440 | tf_op jit(solution)/shard_map/ppermute | solution.py:188
  10.5 9.7 %collective-permute-start.2 = (bf16[512,256]{1,0:T(8,128)(2,1)S(1)}, bf16[512,256]{1,0:T(8,128)(2,1)S(1)}, u32[]{:S(2)}, u32[]{:S(2)}) collective-permute-start(bf16[512,256]{1,0:T(8,128)(2,1)S(1)} %get-tuple-element.18), channel_id=1, source_target_pairs={{0,7},{1,0},{2,1},{3,2},{4,3},{5,4},{6,5},{7,6},{8,9},{9,10},{10,1... | collective-permute-start | bytes 786440 | tf_op jit(solution)/shard_map/ppermute | solution.py:188
  20.8 41.9 %copy-start.2 = (f32[1,1,2,256,256]{4,3,2,1,0:T(8,128)S(1)}, f32[1,1,2,256,256]{4,3,2,1,0:T(8,128)}, u32[]{:S(2)}) copy-start(f32[1,1,2,256,256]{4,3,2,1,0:T(8,128)} %param.19) | copy-start | bytes 1572868
  20.8 41.9 %copy-start.3 = (bf16[1,1,2,256,256]{4,3,2,1,0:T(8,128)(2,1)S(1)}, bf16[1,1,2,256,256]{4,3,2,1,0:T(8,128)(2,1)}, u32[]{:S(2)}) copy-start(bf16[1,1,2,256,256]{4,3,2,1,0:T(8,128)(2,1)} %param.17) | copy-start | bytes 786436
  20.8 41.9 %copy-start.4 = (bf16[1,1,2,256,256]{4,3,2,1,0:T(8,128)(2,1)S(1)}, bf16[1,1,2,256,256]{4,3,2,1,0:T(8,128)(2,1)}, u32[]{:S(2)}) copy-start(bf16[1,1,2,256,256]{4,3,2,1,0:T(8,128)(2,1)} %param.18) | copy-start | bytes 786436
  96.4 16.2 %copy-start.6 = (f32[1,1,2,256,256]{4,3,2,1,0:T(8,128)S(1)}, f32[1,1,2,256,256]{4,3,2,1,0:T(8,128)}, u32[]{:S(2)}) copy-start(f32[1,1,2,256,256]{4,3,2,1,0:T(8,128)} %param.16) | copy-start | bytes 1572868
  96.9 16.8 %copy-start.7 = (f32[1,1,2,256,256]{4,3,2,1,0:T(8,128)S(1)}, f32[1,1,2,256,256]{4,3,2,1,0:T(8,128)}, u32[]{:S(2)}) copy-start(f32[1,1,2,256,256]{4,3,2,1,0:T(8,128)} %param.15) | copy-start | bytes 1572868
  96.9 15.7 %collective-permute-start.3 = (bf16[512,256]{1,0:T(8,128)(2,1)S(1)}, bf16[512,256]{1,0:T(8,128)(2,1)S(1)}, u32[]{:S(2)}, u32[]{:S(2)}) collective-permute-start(bf16[512,256]{1,0:T(8,128)(2,1)S(1)} %shard_map.115.refs_0_), channel_id=1, source_target_pairs={{0,2},{1,3},{2,4},{3,5},{4,6},{5,7},{6,0},{7,1},{8,14},{9,15},{10,... | collective-permute-start | bytes 786440 | tf_op jit(solution)/shard_map/ppermute | solution.py:188
  100.0 14.8 %collective-permute-start.4 = (bf16[512,256]{1,0:T(8,128)(2,1)S(1)}, bf16[512,256]{1,0:T(8,128)(2,1)S(1)}, u32[]{:S(2)}, u32[]{:S(2)}) collective-permute-start(bf16[512,256]{1,0:T(8,128)(2,1)S(1)} %shard_map.115.refs_0_), channel_id=1, source_target_pairs={{0,7},{1,0},{2,1},{3,2},{4,3},{5,4},{6,5},{7,6},{8,9},{9,10},{10,1... | collective-permute-start | bytes 786440 | tf_op jit(solution)/shard_map/ppermute | solution.py:188
  104.4 10.8 %collective-permute-start.5 = (bf16[512,256]{1,0:T(8,128)(2,1)S(1)}, bf16[512,256]{1,0:T(8,128)(2,1)S(1)}, u32[]{:S(2)}, u32[]{:S(2)}) collective-permute-start(bf16[512,256]{1,0:T(8,128)(2,1)S(1)} %shard_map.115.refs_0_), channel_id=1, source_target_pairs={{0,1},{1,2},{2,3},{3,4},{4,5},{5,6},{6,7},{7,0},{8,15},{9,8},{10,9... | collective-permute-start | bytes 786440 | tf_op jit(solution)/shard_map/ppermute | solution.py:188

commit v4 on v3

--- a/solution.py
+++ b/solution.py
@@ -34,13 +34,27 @@
 
 def split_kernel(row_count, halves, grads_ref, *refs):
     rows_at = row_order(row_count)
-    outs, wide = refs[:-1], refs[-1]
+    outs, (near, wide, sems) = refs[:-3], refs[-3:]
     step = row_count * halves
-    wide[...] = grads_ref[...].astype(F32)
-    for n, out in enumerate(outs):
-        for half in range(halves):
-            part = wide[pl.ds(half * row_count + rows_at[n], out.shape[0], stride=step), :]
-            out[:, half * LANES : (half + 1) * LANES] = part.astype(BF16)
+    chunks = sems.shape[0]
+    size = near.shape[0] // chunks
+    copies = []
+    for chunk in range(chunks):
+        span = pl.ds(chunk * size, size)
+        copy = pltpu.make_async_copy(grads_ref.at[span], near.at[span], sems.at[chunk])
+        copy.start()
+        copies.append(copy)
+    for chunk, copy in enumerate(copies):
+        copy.wait()
+        first, last = chunk * size, (chunk + 1) * size
+        wide[first:last, :] = near[first:last, :].astype(F32)
+        for n, out in enumerate(outs):
+            for half in range(halves):
+                start = first + half * row_count + rows_at[n]
+                part = wide[pl.ds(start, size // step, stride=step), :]
+                out[first // step : last // step, half * LANES : (half + 1) * LANES] = part.astype(
+                    BF16
+                )
 
 
 def join_kernel(row_count, halves, *refs):
@@ -80,12 +94,12 @@
             wide[pl.ds(half * slots + slot, owners, stride=halves * slots), :] = rows[
                 :, half * LANES : (half + 1) * LANES
             ]
-    out_ref[...] = wide[...].astype(BF16)
+    out_ref[...] = wide[: out_ref.shape[0], :].astype(BF16)
 
 
 def place_kernel(halves, place_ref, got_ref, out_ref, wide):
     slots, _, owners = place_ref.shape
-    wide[...] = got_ref[...].astype(F32)
+    wide[: got_ref.shape[0], :] = got_ref[...].astype(F32)
     rows = 0.0
     for slot in range(slots):
         parts = [
@@ -106,7 +120,7 @@
     owners = gather_ref.shape[1]
     step = slots * halves
     every = range(slots)
-    wide[...] = got_ref[...].astype(F32)
+    wide[: got_ref.shape[0], :] = got_ref[...].astype(F32)
     row_ids = lax.broadcasted_iota(jnp.int32, (size, size), 0)
     col_ids = lax.broadcasted_iota(jnp.int32, (size, size), 1)
     parts = [
@@ -153,7 +167,7 @@
             wide_out[pl.ds(half * slots + slot, owners, stride=step), :] = rows[
                 :, first : first + LANES
             ]
-    out_ref[...] = wide_out[...].astype(BF16)
+    out_ref[...] = wide_out[: out_ref.shape[0], :].astype(BF16)
 
 
 def body(
@@ -194,9 +208,9 @@
     sent_shape = jax.ShapeDtypeStruct((owners * halves * slot_count, LANES), BF16)
     tile_rows = slab_count * tiles * row_count
     near_grads = pltpu.VMEM((tile_rows, LANES), BF16)
-    wide_grads = pltpu.VMEM((tile_rows, LANES), F32)
+    wide_grads = pltpu.VMEM((tile_rows + row_count * halves, LANES), F32)
     chunk_sems = pltpu.SemaphoreType.DMA((4,))
-    wide_sent = pltpu.VMEM(sent_shape.shape, F32)
+    wide_sent = pltpu.VMEM((sent_shape.shape[0] + 8, LANES), F32)
 
     by_tile = (
         gradients[0]
@@ -207,9 +221,9 @@
     row_zero, row_two, row_one, row_three = call(
         functools.partial(split_kernel, row_count, halves),
         (rows_shape,) * row_count,
-        [wide_grads],
-        [pltpu.VMEM],
-    )(by_tile)
+        [near_grads, wide_grads, chunk_sems],
+        [pltpu.HBM],
+    )(pltpu.with_memory_space_constraint(by_tile, pltpu.HBM))
     from_two = crossed(row_two, 2)
     from_one = crossed(row_one, 1)
     from_three = crossed(row_three, -1)

time: 118 us -> 118 us (level)
  local copies, waits for them, and re-layouts: 2.93 us -> 1.71 us
    unnamed x19 -> x17, local copies, waits for them, and re-layouts: 1.36 us -> 0.14 us
where the time goes in v4:
time: 118 us; the launch traced here: 116 us
  blocking collectives  73.5 us (62%)
  starting transfers between devices  21 us (18%)
  waiting for transfers between devices  10.4 us (9%)
  Pallas kernels  6.01 us (5%)
  matrix products  2.13 us (2%)
  local copies, waits for them, and re-layouts  1.71 us (1%)
    all_to_all x2, blocking collectives, everywhere(): lax.all_to_all(operand, ('fsdp', 'rep'), split_axis=0, concat_axis=0, til...  73.5 us
    ppermute x6, starting transfers between devices, crossed(): return lax.ppermute(operand, ('fsdp', 'rep'), pairs)  21 us
    ppermute x6, waiting for transfers between devices, crossed(): return lax.ppermute(operand, ('fsdp', 'rep'), pairs)  10.4 us
  transfers between devices with their start and end apart: 6, of which 3 were waited for; matrix products, arithmetic and copies ran while one was open for 4% of the time, Pallas kernels for 0%

profile of v4, /device:TPU:6, one launch (start us, length us, event | category | flops | bytes accessed | tf_op | source)
XLA Modules:
  0.0 116.4 jit_solution(8581029649836045879)
XLA Ops:
  0.7 1.6 %shard_map.112 = (bf16[512,256]{1,0:T(8,128)(2,1)S(1)}, bf16[512,256]{1,0:T(8,128)(2,1)S(1)}, bf16[512,256]{1,0:T(8,128)(2,1)S(1)}, bf16[512,256]{1,0:T(8,128)(2,1)S(1)}) custom-call(bf16[4096,128]{1,0:T(8,128)(2,1)} %bitcast.43), custom_call_target="tpu_custom_call" | custom-call | tf_op jit(solution)/shard_map/pallas_call | solution.py:221
  2.3 4.5 %collective-permute-start = (bf16[512,256]{1,0:T(8,128)(2,1)S(1)}, bf16[512,256]{1,0:T(8,128)(2,1)S(1)}, u32[]{:S(2)}, u32[]{:S(2)}) collective-permute-start(bf16[512,256]{1,0:T(8,128)(2,1)S(1)} %get-tuple-element.16), channel_id=1, source_target_pairs={{0,2},{1,3},{2,4},{3,5},{4,6},{5,7},{6,0},{7,1},{8,14},{9,15},{10,... | collective-permute-start | bytes 786440 | tf_op jit(solution)/shard_map/ppermute | solution.py:202
  6.8 3.5 %collective-permute-start.1 = (bf16[512,256]{1,0:T(8,128)(2,1)S(1)}, bf16[512,256]{1,0:T(8,128)(2,1)S(1)}, u32[]{:S(2)}, u32[]{:S(2)}) collective-permute-start(bf16[512,256]{1,0:T(8,128)(2,1)S(1)} %get-tuple-element.17), channel_id=1, source_target_pairs={{0,1},{1,2},{2,3},{3,4},{4,5},{5,6},{6,7},{7,0},{8,15},{9,8},{10,9... | collective-permute-start | bytes 786440 | tf_op jit(solution)/shard_map/ppermute | solution.py:202
  10.3 3.6 %collective-permute-start.2 = (bf16[512,256]{1,0:T(8,128)(2,1)S(1)}, bf16[512,256]{1,0:T(8,128)(2,1)S(1)}, u32[]{:S(2)}, u32[]{:S(2)}) collective-permute-start(bf16[512,256]{1,0:T(8,128)(2,1)S(1)} %get-tuple-element.18), channel_id=1, source_target_pairs={{0,7},{1,0},{2,1},{3,2},{4,3},{5,4},{6,5},{7,6},{8,9},{9,10},{10,1... | collective-permute-start | bytes 786440 | tf_op jit(solution)/shard_map/ppermute | solution.py:202
  14.0 0.1 reshape.137
  14.1 0.2 dynamic-slice_reduce_fusion
  14.3 0.6 gather_fusion
  15.0 0.6 gather_fusion.1
  15.6 0.1 and_convert_fusion.gather_ref
  15.8 0.6 fusion.1
  16.4 3.7 %collective-permute-done.1.one_ref = bf16[512,256]{1,0:T(8,128)(2,1)S(1)} collective-permute-done((bf16[512,256]{1,0:T(8,128)(2,1)S(1)}, bf16[512,256]{1,0:T(8,128)(2,1)S(1)}, u32[]{:S(2)}, u32[]{:S(2)}) %collective-permute-start.1) | collective-permute-done | bytes 262176 | tf_op jit(solution)/shard_map/ppermute | solution.py:202
  20.0 0.5 shard_map.113
  20.6 41.8 %all_to_all.22 = bf16[512,4,128]{2,1,0:T(4,128)(2,1)S(1)} all-to-all(bf16[512,4,128]{2,1,0:T(4,128)(2,1)S(1)} %bitcast.36), channel_id=1, replica_groups=mesh['fsdp'=64,'rep'=8] {'fsdp','rep'}, dimensions={0} | all-to-all | bytes 1048576 | tf_op jit(solution)/shard_map/all_to_all | solution.py:205
  62.5 2.0 %shard_map.114 = (bf16[2,256,256]{2,1,0:T(8,128)(2,1)S(1)}, bf16[2048,128]{1,0:T(8,128)(2,1)S(1)}) custom-call(s32[2,2]{1,0:T(2,128)S(1)} %pad_add_fusion.limits_ref, bf16[256,512]{1,0:T(8,128)(2,1)S(1)} %and_convert_fusion.gather_ref, bf16[2048,128]{1,0:T(8,128)(2,1)S(1)} %bitcast.37, bf16[2,256,256]{2,1,0:T(8,128)(2,1)S(1)} %bitcast.41, ...), custom_call_target="tpu_custom_call" | custom-call | tf_op jit(solution)/shard_map/pallas_call | solution.py:248
  64.5 31.7 %all_to_all.23 = bf16[512,4,128]{2,1,0:T(4,128)(2,1)S(1)} all-to-all(bf16[512,4,128]{2,1,0:T(4,128)(2,1)S(1)} %bitcast.40), channel_id=1, replica_groups=mesh['fsdp'=64,'rep'=8] {'fsdp','rep'}, dimensions={0} | all-to-all | bytes 1048576 | tf_op jit(solution)/shard_map/all_to_all | solution.py:205
  96.2 0.5 shard_map.115.refs_0_
  96.6 3.1 %collective-permute-start.3 = (bf16[512,256]{1,0:T(8,128)(2,1)S(1)}, bf16[512,256]{1,0:T(8,128)(2,1)S(1)}, u32[]{:S(2)}, u32[]{:S(2)}) collective-permute-start(bf16[512,256]{1,0:T(8,128)(2,1)S(1)} %shard_map.115.refs_0_), channel_id=1, source_target_pairs={{0,2},{1,3},{2,4},{3,5},{4,6},{5,7},{6,0},{7,1},{8,14},{9,15},{10,... | collective-permute-start | bytes 786440 | tf_op jit(solution)/shard_map/ppermute | solution.py:202
  99.7 4.4 %collective-permute-start.4 = (bf16[512,256]{1,0:T(8,128)(2,1)S(1)}, bf16[512,256]{1,0:T(8,128)(2,1)S(1)}, u32[]{:S(2)}, u32[]{:S(2)}) collective-permute-start(bf16[512,256]{1,0:T(8,128)(2,1)S(1)} %shard_map.115.refs_0_), channel_id=1, source_target_pairs={{0,7},{1,0},{2,1},{3,2},{4,3},{5,4},{6,5},{7,6},{8,9},{9,10},{10,1... | collective-permute-start | bytes 786440 | tf_op jit(solution)/shard_map/ppermute | solution.py:202
  104.2 1.9 %collective-permute-start.5 = (bf16[512,256]{1,0:T(8,128)(2,1)S(1)}, bf16[512,256]{1,0:T(8,128)(2,1)S(1)}, u32[]{:S(2)}, u32[]{:S(2)}) collective-permute-start(bf16[512,256]{1,0:T(8,128)(2,1)S(1)} %shard_map.115.refs_0_), channel_id=1, source_target_pairs={{0,1},{1,2},{2,3},{3,4},{4,5},{5,6},{6,7},{7,0},{8,15},{9,8},{10,9... | collective-permute-start | bytes 786440 | tf_op jit(solution)/shard_map/ppermute | solution.py:202
  106.1 6.3 %collective-permute-done.3.refs_1_ = bf16[512,256]{1,0:T(8,128)(2,1)S(1)} collective-permute-done((bf16[512,256]{1,0:T(8,128)(2,1)S(1)}, bf16[512,256]{1,0:T(8,128)(2,1)S(1)}, u32[]{:S(2)}, u32[]{:S(2)}) %collective-permute-start.3) | collective-permute-done | bytes 262176 | tf_op jit(solution)/shard_map/ppermute | solution.py:202
  112.4 1.1 fusion.3
  113.5 1.1 fusion.5
  114.5 0.5 collective-permute-done.5.refs_3_
  115.0 1.4 %shard_map.116 = bf16[4096,128]{1,0:T(8,128)(2,1)} custom-call(bf16[512,256]{1,0:T(8,128)(2,1)S(1)} %shard_map.115.refs_0_, bf16[512,256]{1,0:T(8,128)(2,1)S(1)} %collective-permute-done.3.refs_1_, bf16[512,256]{1,0:T(8,128)(2,1)S(1)} %collective-permute-done.4.refs_2_, bf16[512,256]{1,0:T(8,128)(2,1)S(1)} %collective-permute-done.5.refs_3_), custom_call_target="tpu_custom_call" | custom-call | tf_op jit(solution)/shard_map/pallas_call | solution.py:275
  (26 shorter events, 0.2 us)
Async XLA Ops:
  0.6 13.7 %copy-start = (s32[512]{0:T(512)S(1)}, s32[512]{0:T(512)}, u32[]{:S(2)}) copy-start(s32[512]{0:T(512)} %param.13) | copy-start | bytes 6148
  0.6 13.2 %copy-start.7 = (s32[64,8,2]{0,2,1:T(2,128)S(1)}, s32[64,8,2]{0,2,1:T(2,128)}, u32[]{:S(2)}) copy-start(s32[64,8,2]{0,2,1:T(2,128)} %param.12) | copy-start | bytes 12292
  0.7 14.3 %copy-start.4 = (s32[512]{0:T(512)S(1)}, s32[512]{0:T(512)}, u32[]{:S(2)}) copy-start(s32[512]{0:T(512)} %param.14) | copy-start | bytes 6148
  2.3 14.1 %collective-permute-start = (bf16[512,256]{1,0:T(8,128)(2,1)S(1)}, bf16[512,256]{1,0:T(8,128)(2,1)S(1)}, u32[]{:S(2)}, u32[]{:S(2)}) collective-permute-start(bf16[512,256]{1,0:T(8,128)(2,1)S(1)} %get-tuple-element.16), channel_id=1, source_target_pairs={{0,2},{1,3},{2,4},{3,5},{4,6},{5,7},{6,0},{7,1},{8,14},{9,15},{10,... | collective-permute-start | bytes 786440 | tf_op jit(solution)/shard_map/ppermute | solution.py:202
  6.8 13.2 %collective-permute-start.1 = (bf16[512,256]{1,0:T(8,128)(2,1)S(1)}, bf16[512,256]{1,0:T(8,128)(2,1)S(1)}, u32[]{:S(2)}, u32[]{:S(2)}) collective-permute-start(bf16[512,256]{1,0:T(8,128)(2,1)S(1)} %get-tuple-element.17), channel_id=1, source_target_pairs={{0,1},{1,2},{2,3},{3,4},{4,5},{5,6},{6,7},{7,0},{8,15},{9,8},{10,9... | collective-permute-start | bytes 786440 | tf_op jit(solution)/shard_map/ppermute | solution.py:202
  10.3 9.7 %collective-permute-start.2 = (bf16[512,256]{1,0:T(8,128)(2,1)S(1)}, bf16[512,256]{1,0:T(8,128)(2,1)S(1)}, u32[]{:S(2)}, u32[]{:S(2)}) collective-permute-start(bf16[512,256]{1,0:T(8,128)(2,1)S(1)} %get-tuple-element.18), channel_id=1, source_target_pairs={{0,7},{1,0},{2,1},{3,2},{4,3},{5,4},{6,5},{7,6},{8,9},{9,10},{10,1... | collective-permute-start | bytes 786440 | tf_op jit(solution)/shard_map/ppermute | solution.py:202
  20.6 41.9 %copy-start.1 = (f32[1,1,2,256,256]{4,3,2,1,0:T(8,128)S(1)}, f32[1,1,2,256,256]{4,3,2,1,0:T(8,128)}, u32[]{:S(2)}) copy-start(f32[1,1,2,256,256]{4,3,2,1,0:T(8,128)} %param.19) | copy-start | bytes 1572868
  20.6 41.9 %copy-start.2 = (bf16[1,1,2,256,256]{4,3,2,1,0:T(8,128)(2,1)S(1)}, bf16[1,1,2,256,256]{4,3,2,1,0:T(8,128)(2,1)}, u32[]{:S(2)}) copy-start(bf16[1,1,2,256,256]{4,3,2,1,0:T(8,128)(2,1)} %param.17) | copy-start | bytes 786436
  20.6 41.9 %copy-start.3 = (bf16[1,1,2,256,256]{4,3,2,1,0:T(8,128)(2,1)S(1)}, bf16[1,1,2,256,256]{4,3,2,1,0:T(8,128)(2,1)}, u32[]{:S(2)}) copy-start(bf16[1,1,2,256,256]{4,3,2,1,0:T(8,128)(2,1)} %param.18) | copy-start | bytes 786436
  96.1 16.2 %copy-start.5 = (f32[1,1,2,256,256]{4,3,2,1,0:T(8,128)S(1)}, f32[1,1,2,256,256]{4,3,2,1,0:T(8,128)}, u32[]{:S(2)}) copy-start(f32[1,1,2,256,256]{4,3,2,1,0:T(8,128)} %param.16) | copy-start | bytes 1572868
  96.6 16.8 %copy-start.6 = (f32[1,1,2,256,256]{4,3,2,1,0:T(8,128)S(1)}, f32[1,1,2,256,256]{4,3,2,1,0:T(8,128)}, u32[]{:S(2)}) copy-start(f32[1,1,2,256,256]{4,3,2,1,0:T(8,128)} %param.15) | copy-start | bytes 1572868
  96.6 15.7 %collective-permute-start.3 = (bf16[512,256]{1,0:T(8,128)(2,1)S(1)}, bf16[512,256]{1,0:T(8,128)(2,1)S(1)}, u32[]{:S(2)}, u32[]{:S(2)}) collective-permute-start(bf16[512,256]{1,0:T(8,128)(2,1)S(1)} %shard_map.115.refs_0_), channel_id=1, source_target_pairs={{0,2},{1,3},{2,4},{3,5},{4,6},{5,7},{6,0},{7,1},{8,14},{9,15},{10,... | collective-permute-start | bytes 786440 | tf_op jit(solution)/shard_map/ppermute | solution.py:202
  99.7 14.8 %collective-permute-start.4 = (bf16[512,256]{1,0:T(8,128)(2,1)S(1)}, bf16[512,256]{1,0:T(8,128)(2,1)S(1)}, u32[]{:S(2)}, u32[]{:S(2)}) collective-permute-start(bf16[512,256]{1,0:T(8,128)(2,1)S(1)} %shard_map.115.refs_0_), channel_id=1, source_target_pairs={{0,7},{1,0},{2,1},{3,2},{4,3},{5,4},{6,5},{7,6},{8,9},{9,10},{10,1... | collective-permute-start | bytes 786440 | tf_op jit(solution)/shard_map/ppermute | solution.py:202
  104.2 10.8 %collective-permute-start.5 = (bf16[512,256]{1,0:T(8,128)(2,1)S(1)}, bf16[512,256]{1,0:T(8,128)(2,1)S(1)}, u32[]{:S(2)}, u32[]{:S(2)}) collective-permute-start(bf16[512,256]{1,0:T(8,128)(2,1)S(1)} %shard_map.115.refs_0_), channel_id=1, source_target_pairs={{0,1},{1,2},{2,3},{3,4},{4,5},{5,6},{6,7},{7,0},{8,15},{9,8},{10,9... | collective-permute-start | bytes 786440 | tf_op jit(solution)/shard_map/ppermute | solution.py:202

commit v5 on v4

--- a/solution.py
+++ b/solution.py
@@ -170,6 +170,24 @@
     out_ref[...] = wide_out[: out_ref.shape[0], :].astype(BF16)
 
 
+def factor_kernel(grad_ref, left_ref, right_ref, left_out, right_out, left, right, sems):
+    copies = []
+    for slot in range(grad_ref.shape[0]):
+        grad = grad_ref[slot]
+        for side, (old, new, out) in enumerate(
+            ((left_ref, left, left_out), (right_ref, right, right_out))
+        ):
+            product = lax.dot_general(
+                grad, grad, (((1 - side,), (1 - side,)), ((), ())), preferred_element_type=F32
+            )
+            new[slot] = factor_decay * old[slot] + (1.0 - factor_decay) * product
+            copy = pltpu.make_async_copy(new.at[slot], out.at[slot], sems.at[2 * slot + side])
+            copy.start()
+            copies.append(copy)
+    for copy in copies:
+        copy.wait()
+
+
 def body(
     gradients,
     owned_blocks,
@@ -209,7 +227,7 @@
     tile_rows = slab_count * tiles * row_count
     near_grads = pltpu.VMEM((tile_rows, LANES), BF16)
     wide_grads = pltpu.VMEM((tile_rows + row_count * halves, LANES), F32)
-    chunk_sems = pltpu.SemaphoreType.DMA((4,))
+    chunk_sems = pltpu.SemaphoreType.DMA((8,))
     wide_sent = pltpu.VMEM((sent_shape.shape[0] + 8, LANES), F32)
 
     by_tile = (
@@ -266,12 +284,15 @@
     row_one = crossed(placed, 1)
     row_three = crossed(placed, -1)
     row_two, grad_block = lax.optimization_barrier((row_two, grad_block))
-    left_next = factor_decay * left_factor[0, 0] + (1.0 - factor_decay) * jnp.einsum(
-        "kij,klj->kil", grad_block, grad_block, preferred_element_type=F32
-    )
-    right_next = factor_decay * right_factor[0, 0] + (1.0 - factor_decay) * jnp.einsum(
-        "kji,kjl->kil", grad_block, grad_block, preferred_element_type=F32
-    )
+    factors_shape = jax.ShapeDtypeStruct((slot_count, size_b, size_b), F32)
+    factors_scratch = pltpu.VMEM((slot_count, size_b, size_b), F32)
+    left_next, right_next = call(
+        factor_kernel,
+        (factors_shape, factors_shape),
+        [factors_scratch, factors_scratch, pltpu.SemaphoreType.DMA((2 * slot_count,))],
+        [pltpu.VMEM] * 3,
+        out_space=pltpu.HBM,
+    )(grad_block, left_factor[0, 0], right_factor[0, 0])
     joined = call(
         functools.partial(join_kernel, row_count, halves),
         jax.ShapeDtypeStruct((tile_rows, LANES), BF16),

time: 118 us -> 118 us (level)
  matrix products: 2.13 us -> 0 us
  Pallas kernels: 6.01 us -> 7.28 us
    dot_general x2 -> x0, matrix products: 2.13 us -> none  [the longest x1 1.08 us: body(): jnp.einsum('kji,kjl->kil', grad_block, grad_block, preferred_element_type...]
    pallas_call x0 -> x1, Pallas kernels: none -> 1.26 us  [body(): call(factor_kernel, (factors_shape, factors_shape), [factors_scratch, fac...]
  transfers between devices with their start and end apart: 6 -> 6, of which waited for: 3 -> 3; matrix products, arithmetic and copies ran while one was open for 4% -> 2% of each run, Pallas kernels for 0% -> 1%
where the time goes in v5:
time: 118 us; the launch traced here: 116 us
  blocking collectives  73.5 us (62%)
  starting transfers between devices  20.8 us (18%)
  waiting for transfers between devices  11.3 us (10%)
  Pallas kernels  7.28 us (6%)
  local copies, waits for them, and re-layouts  1.7 us (1%)
    all_to_all x2, blocking collectives, everywhere(): lax.all_to_all(operand, ('fsdp', 'rep'), split_axis=0, concat_axis=0, til...  73.5 us
    ppermute x6, starting transfers between devices, crossed(): return lax.ppermute(operand, ('fsdp', 'rep'), pairs)  20.8 us
    ppermute x6, waiting for transfers between devices, crossed(): return lax.ppermute(operand, ('fsdp', 'rep'), pairs)  11.3 us
  transfers between devices with their start and end apart: 6, of which 3 were waited for; matrix products, arithmetic and copies ran while one was open for 2% of the time, Pallas kernels for 1%

profile of v5, /device:TPU:6, one launch (start us, length us, event | category | flops | bytes accessed | tf_op | source)
XLA Modules:
  0.0 116.2 jit_solution(6333141010139075337)
XLA Ops:
  0.7 1.6 %shard_map.112 = (bf16[512,256]{1,0:T(8,128)(2,1)S(1)}, bf16[512,256]{1,0:T(8,128)(2,1)S(1)}, bf16[512,256]{1,0:T(8,128)(2,1)S(1)}, bf16[512,256]{1,0:T(8,128)(2,1)S(1)}) custom-call(bf16[4096,128]{1,0:T(8,128)(2,1)} %bitcast.37), custom_call_target="tpu_custom_call" | custom-call | tf_op jit(solution)/shard_map/pallas_call | solution.py:239
  2.3 4.5 %collective-permute-start = (bf16[512,256]{1,0:T(8,128)(2,1)S(1)}, bf16[512,256]{1,0:T(8,128)(2,1)S(1)}, u32[]{:S(2)}, u32[]{:S(2)}) collective-permute-start(bf16[512,256]{1,0:T(8,128)(2,1)S(1)} %get-tuple-element.18), channel_id=1, source_target_pairs={{0,2},{1,3},{2,4},{3,5},{4,6},{5,7},{6,0},{7,1},{8,14},{9,15},{10,... | collective-permute-start | bytes 786440 | tf_op jit(solution)/shard_map/ppermute | solution.py:220
  6.8 3.5 %collective-permute-start.1 = (bf16[512,256]{1,0:T(8,128)(2,1)S(1)}, bf16[512,256]{1,0:T(8,128)(2,1)S(1)}, u32[]{:S(2)}, u32[]{:S(2)}) collective-permute-start(bf16[512,256]{1,0:T(8,128)(2,1)S(1)} %get-tuple-element.19), channel_id=1, source_target_pairs={{0,1},{1,2},{2,3},{3,4},{4,5},{5,6},{6,7},{7,0},{8,15},{9,8},{10,9... | collective-permute-start | bytes 786440 | tf_op jit(solution)/shard_map/ppermute | solution.py:220
  10.3 3.6 %collective-permute-start.2 = (bf16[512,256]{1,0:T(8,128)(2,1)S(1)}, bf16[512,256]{1,0:T(8,128)(2,1)S(1)}, u32[]{:S(2)}, u32[]{:S(2)}) collective-permute-start(bf16[512,256]{1,0:T(8,128)(2,1)S(1)} %get-tuple-element.20), channel_id=1, source_target_pairs={{0,7},{1,0},{2,1},{3,2},{4,3},{5,4},{6,5},{7,6},{8,9},{9,10},{10,1... | collective-permute-start | bytes 786440 | tf_op jit(solution)/shard_map/ppermute | solution.py:220
  13.9 0.1 copy.14
  14.0 0.1 reshape.133
  14.1 0.2 dynamic-slice_reduce_fusion
  14.3 0.6 gather_fusion
  15.0 0.6 gather_fusion.1
  15.6 0.1 and_convert_fusion.gather_ref
  15.8 0.6 fusion.1
  16.4 3.7 %collective-permute-done.1.one_ref = bf16[512,256]{1,0:T(8,128)(2,1)S(1)} collective-permute-done((bf16[512,256]{1,0:T(8,128)(2,1)S(1)}, bf16[512,256]{1,0:T(8,128)(2,1)S(1)}, u32[]{:S(2)}, u32[]{:S(2)}) %collective-permute-start.1) | collective-permute-done | bytes 262176 | tf_op jit(solution)/shard_map/ppermute | solution.py:220
  20.1 0.5 shard_map.113
  20.6 41.8 %all_to_all.22 = bf16[512,4,128]{2,1,0:T(4,128)(2,1)S(1)} all-to-all(bf16[512,4,128]{2,1,0:T(4,128)(2,1)S(1)} %bitcast.28), channel_id=1, replica_groups=mesh['fsdp'=64,'rep'=8] {'fsdp','rep'}, dimensions={0} | all-to-all | bytes 1048576 | tf_op jit(solution)/shard_map/all_to_all | solution.py:223
  62.5 2.0 %shard_map.114 = (bf16[2,256,256]{2,1,0:T(8,128)(2,1)S(1)}, bf16[2048,128]{1,0:T(8,128)(2,1)S(1)}) custom-call(s32[2,2]{1,0:T(2,128)S(1)} %pad_add_fusion.limits_ref, bf16[256,512]{1,0:T(8,128)(2,1)S(1)} %and_convert_fusion.gather_ref, bf16[2048,128]{1,0:T(8,128)(2,1)S(1)} %bitcast.29, bf16[2,256,256]{2,1,0:T(8,128)(2,1)S(1)} %bitcast.35, ...), custom_call_target="tpu_custom_call" | custom-call | tf_op jit(solution)/shard_map/pallas_call | solution.py:266
  64.5 31.7 %all_to_all.23 = bf16[512,4,128]{2,1,0:T(4,128)(2,1)S(1)} all-to-all(bf16[512,4,128]{2,1,0:T(4,128)(2,1)S(1)} %bitcast.34), channel_id=1, replica_groups=mesh['fsdp'=64,'rep'=8] {'fsdp','rep'}, dimensions={0} | all-to-all | bytes 1048576 | tf_op jit(solution)/shard_map/all_to_all | solution.py:223
  96.2 0.5 shard_map.115.refs_0_
  96.7 2.9 %collective-permute-start.3 = (bf16[512,256]{1,0:T(8,128)(2,1)S(1)}, bf16[512,256]{1,0:T(8,128)(2,1)S(1)}, u32[]{:S(2)}, u32[]{:S(2)}) collective-permute-start(bf16[512,256]{1,0:T(8,128)(2,1)S(1)} %shard_map.115.refs_0_), channel_id=1, source_target_pairs={{0,2},{1,3},{2,4},{3,5},{4,6},{5,7},{6,0},{7,1},{8,14},{9,15},{10,... | collective-permute-start | bytes 786440 | tf_op jit(solution)/shard_map/ppermute | solution.py:220
  99.6 4.4 %collective-permute-start.4 = (bf16[512,256]{1,0:T(8,128)(2,1)S(1)}, bf16[512,256]{1,0:T(8,128)(2,1)S(1)}, u32[]{:S(2)}, u32[]{:S(2)}) collective-permute-start(bf16[512,256]{1,0:T(8,128)(2,1)S(1)} %shard_map.115.refs_0_), channel_id=1, source_target_pairs={{0,7},{1,0},{2,1},{3,2},{4,3},{5,4},{6,5},{7,6},{8,9},{9,10},{10,1... | collective-permute-start | bytes 786440 | tf_op jit(solution)/shard_map/ppermute | solution.py:220
  104.1 1.9 %collective-permute-start.5 = (bf16[512,256]{1,0:T(8,128)(2,1)S(1)}, bf16[512,256]{1,0:T(8,128)(2,1)S(1)}, u32[]{:S(2)}, u32[]{:S(2)}) collective-permute-start(bf16[512,256]{1,0:T(8,128)(2,1)S(1)} %shard_map.115.refs_0_), channel_id=1, source_target_pairs={{0,1},{1,2},{2,3},{3,4},{4,5},{5,6},{6,7},{7,0},{8,15},{9,8},{10,9... | collective-permute-start | bytes 786440 | tf_op jit(solution)/shard_map/ppermute | solution.py:220
  106.0 6.3 %collective-permute-done.3.refs_1_ = bf16[512,256]{1,0:T(8,128)(2,1)S(1)} collective-permute-done((bf16[512,256]{1,0:T(8,128)(2,1)S(1)}, bf16[512,256]{1,0:T(8,128)(2,1)S(1)}, u32[]{:S(2)}, u32[]{:S(2)}) %collective-permute-start.3) | collective-permute-done | bytes 262176 | tf_op jit(solution)/shard_map/ppermute | solution.py:220
  112.3 1.3 %shard_map.117 = (f32[2,256,256]{2,1,0:T(8,128)}, f32[2,256,256]{2,1,0:T(8,128)}) custom-call(bf16[2,256,256]{2,1,0:T(8,128)(2,1)S(1)} %get-tuple-element.27.grad_ref, f32[2,256,256]{2,1,0:T(8,128)S(1)} %bitcast.32, f32[2,256,256]{2,1,0:T(8,128)S(1)} %bitcast.33), custom_call_target="tpu_custom_call" | custom-call | tf_op jit(solution)/shard_map/pallas_call | solution.py:289
  113.5 1.3 %collective-permute-done.5.refs_3_ = bf16[512,256]{1,0:T(8,128)(2,1)S(1)} collective-permute-done((bf16[512,256]{1,0:T(8,128)(2,1)S(1)}, bf16[512,256]{1,0:T(8,128)(2,1)S(1)}, u32[]{:S(2)}, u32[]{:S(2)}) %collective-permute-start.5) | collective-permute-done | bytes 262176 | tf_op jit(solution)/shard_map/ppermute | solution.py:220
  114.9 1.4 %shard_map.116 = bf16[4096,128]{1,0:T(8,128)(2,1)} custom-call(bf16[512,256]{1,0:T(8,128)(2,1)S(1)} %shard_map.115.refs_0_, bf16[512,256]{1,0:T(8,128)(2,1)S(1)} %collective-permute-done.3.refs_1_, bf16[512,256]{1,0:T(8,128)(2,1)S(1)} %collective-permute-done.4.refs_2_, bf16[512,256]{1,0:T(8,128)(2,1)S(1)} %collective-permute-done.5.refs_3_), custom_call_target="tpu_custom_call" | custom-call | tf_op jit(solution)/shard_map/pallas_call | solution.py:296
  (25 shorter events, 0.1 us)
Async XLA Ops:
  0.6 13.7 %copy-start = (s32[512]{0:T(512)S(1)}, s32[512]{0:T(512)}, u32[]{:S(2)}) copy-start(s32[512]{0:T(512)} %param.13) | copy-start | bytes 6148
  0.6 13.3 %copy-start.7 = (s32[64,8,2]{0,2,1:T(2,128)S(1)}, s32[64,8,2]{0,2,1:T(2,128)}, u32[]{:S(2)}) copy-start(s32[64,8,2]{0,2,1:T(2,128)} %param.12) | copy-start | bytes 12292
  0.7 14.3 %copy-start.6 = (s32[512]{0:T(512)S(1)}, s32[512]{0:T(512)}, u32[]{:S(2)}) copy-start(s32[512]{0:T(512)} %param.14) | copy-start | bytes 6148
  2.3 14.1 %collective-permute-start = (bf16[512,256]{1,0:T(8,128)(2,1)S(1)}, bf16[512,256]{1,0:T(8,128)(2,1)S(1)}, u32[]{:S(2)}, u32[]{:S(2)}) collective-permute-start(bf16[512,256]{1,0:T(8,128)(2,1)S(1)} %get-tuple-element.18), channel_id=1, source_target_pairs={{0,2},{1,3},{2,4},{3,5},{4,6},{5,7},{6,0},{7,1},{8,14},{9,15},{10,... | collective-permute-start | bytes 786440 | tf_op jit(solution)/shard_map/ppermute | solution.py:220
  6.8 13.2 %collective-permute-start.1 = (bf16[512,256]{1,0:T(8,128)(2,1)S(1)}, bf16[512,256]{1,0:T(8,128)(2,1)S(1)}, u32[]{:S(2)}, u32[]{:S(2)}) collective-permute-start(bf16[512,256]{1,0:T(8,128)(2,1)S(1)} %get-tuple-element.19), channel_id=1, source_target_pairs={{0,1},{1,2},{2,3},{3,4},{4,5},{5,6},{6,7},{7,0},{8,15},{9,8},{10,9... | collective-permute-start | bytes 786440 | tf_op jit(solution)/shard_map/ppermute | solution.py:220
  10.3 9.7 %collective-permute-start.2 = (bf16[512,256]{1,0:T(8,128)(2,1)S(1)}, bf16[512,256]{1,0:T(8,128)(2,1)S(1)}, u32[]{:S(2)}, u32[]{:S(2)}) collective-permute-start(bf16[512,256]{1,0:T(8,128)(2,1)S(1)} %get-tuple-element.20), channel_id=1, source_target_pairs={{0,7},{1,0},{2,1},{3,2},{4,3},{5,4},{6,5},{7,6},{8,9},{9,10},{10,1... | collective-permute-start | bytes 786440 | tf_op jit(solution)/shard_map/ppermute | solution.py:220
  20.6 41.9 %copy-start.1 = (f32[1,1,2,256,256]{4,3,2,1,0:T(8,128)S(1)}, f32[1,1,2,256,256]{4,3,2,1,0:T(8,128)}, u32[]{:S(2)}) copy-start(f32[1,1,2,256,256]{4,3,2,1,0:T(8,128)} %param.19) | copy-start | bytes 1572868
  20.6 41.9 %copy-start.4 = (bf16[1,1,2,256,256]{4,3,2,1,0:T(8,128)(2,1)S(1)}, bf16[1,1,2,256,256]{4,3,2,1,0:T(8,128)(2,1)}, u32[]{:S(2)}) copy-start(bf16[1,1,2,256,256]{4,3,2,1,0:T(8,128)(2,1)} %param.17) | copy-start | bytes 786436
  20.6 41.9 %copy-start.5 = (bf16[1,1,2,256,256]{4,3,2,1,0:T(8,128)(2,1)S(1)}, bf16[1,1,2,256,256]{4,3,2,1,0:T(8,128)(2,1)}, u32[]{:S(2)}) copy-start(bf16[1,1,2,256,256]{4,3,2,1,0:T(8,128)(2,1)} %param.18) | copy-start | bytes 786436
  96.2 16.1 %copy-start.2 = (f32[1,1,2,256,256]{4,3,2,1,0:T(8,128)S(1)}, f32[1,1,2,256,256]{4,3,2,1,0:T(8,128)}, u32[]{:S(2)}) copy-start(f32[1,1,2,256,256]{4,3,2,1,0:T(8,128)} %param.15) | copy-start | bytes 1572868
  96.2 16.1 %copy-start.3 = (f32[1,1,2,256,256]{4,3,2,1,0:T(8,128)S(1)}, f32[1,1,2,256,256]{4,3,2,1,0:T(8,128)}, u32[]{:S(2)}) copy-start(f32[1,1,2,256,256]{4,3,2,1,0:T(8,128)} %param.16) | copy-start | bytes 1572868
  96.7 15.6 %collective-permute-start.3 = (bf16[512,256]{1,0:T(8,128)(2,1)S(1)}, bf16[512,256]{1,0:T(8,128)(2,1)S(1)}, u32[]{:S(2)}, u32[]{:S(2)}) collective-permute-start(bf16[512,256]{1,0:T(8,128)(2,1)S(1)} %shard_map.115.refs_0_), channel_id=1, source_target_pairs={{0,2},{1,3},{2,4},{3,5},{4,6},{5,7},{6,0},{7,1},{8,14},{9,15},{10,... | collective-permute-start | bytes 786440 | tf_op jit(solution)/shard_map/ppermute | solution.py:220
  99.6 13.9 %collective-permute-start.4 = (bf16[512,256]{1,0:T(8,128)(2,1)S(1)}, bf16[512,256]{1,0:T(8,128)(2,1)S(1)}, u32[]{:S(2)}, u32[]{:S(2)}) collective-permute-start(bf16[512,256]{1,0:T(8,128)(2,1)S(1)} %shard_map.115.refs_0_), channel_id=1, source_target_pairs={{0,7},{1,0},{2,1},{3,2},{4,3},{5,4},{6,5},{7,6},{8,9},{9,10},{10,1... | collective-permute-start | bytes 786440 | tf_op jit(solution)/shard_map/ppermute | solution.py:220
  104.1 10.8 %collective-permute-start.5 = (bf16[512,256]{1,0:T(8,128)(2,1)S(1)}, bf16[512,256]{1,0:T(8,128)(2,1)S(1)}, u32[]{:S(2)}, u32[]{:S(2)}) collective-permute-start(bf16[512,256]{1,0:T(8,128)(2,1)S(1)} %shard_map.115.refs_0_), channel_id=1, source_target_pairs={{0,1},{1,2},{2,3},{3,4},{4,5},{5,6},{6,7},{7,0},{8,15},{9,8},{10,9... | collective-permute-start | bytes 786440 | tf_op jit(solution)/shard_map/ppermute | solution.py:220

commit v6 on v5

--- a/solution.py
+++ b/solution.py
@@ -138,6 +138,11 @@
         wides.append(jnp.where(inside[slot], block, 0.0))
         grads.append(wides[slot].astype(BF16))
         grad_ref[slot] = grads[slot]
+    adam_norms = []
+    for slot, grad_wide in enumerate(wides):
+        moment = moment_decay * moment_ref[slot] + (1.0 - moment_decay) * grad_wide * grad_wide
+        adam = grad_wide / (jnp.sqrt(moment) + adam_eps)
+        adam_norms.append(jnp.sqrt(jnp.sum(adam * adam, axis=(0, 1), keepdims=True)))
     halfway = [
         jnp.dot(lroot_ref[slot], grads[slot], preferred_element_type=F32).astype(BF16)
         for slot in every
@@ -149,10 +154,7 @@
         for slot in every
     ]
     updates = []
-    for slot, (grad_wide, precond) in enumerate(zip(wides, preconds)):
-        moment = moment_decay * moment_ref[slot] + (1.0 - moment_decay) * grad_wide * grad_wide
-        adam = grad_wide / (jnp.sqrt(moment) + adam_eps)
-        adam_norm = jnp.sqrt(jnp.sum(adam * adam, axis=(0, 1), keepdims=True))
+    for adam_norm, precond in zip(adam_norms, preconds):
         pre_norm = jnp.sqrt(jnp.sum(precond * precond, axis=(0, 1), keepdims=True) + 1e-06)
         updates.append((precond * (adam_norm / pre_norm)).astype(BF16))
     rows = lax.dot_general(

time: 118 us -> 118 us (level)
  no operation moved by 1% of the time
where the time goes in v6:
time: 118 us; the launch traced here: 116 us
  blocking collectives  73.5 us (62%)
  starting transfers between devices  20.8 us (18%)
  waiting for transfers between devices  11.3 us (10%)
  Pallas kernels  7.28 us (6%)
  local copies, waits for them, and re-layouts  1.7 us (1%)
    all_to_all x2, blocking collectives, everywhere(): lax.all_to_all(operand, ('fsdp', 'rep'), split_axis=0, concat_axis=0, til...  73.5 us
    ppermute x6, starting transfers between devices, crossed(): return lax.ppermute(operand, ('fsdp', 'rep'), pairs)  20.8 us
    ppermute x6, waiting for transfers between devices, crossed(): return lax.ppermute(operand, ('fsdp', 'rep'), pairs)  11.3 us
  transfers between devices with their start and end apart: 6, of which 3 were waited for; matrix products, arithmetic and copies ran while one was open for 2% of the time, Pallas kernels for 1%

profile of v6, /device:TPU:6, one launch (start us, length us, event | category | flops | bytes accessed | tf_op | source)
XLA Modules:
  0.0 116.3 jit_solution(5742347767561281079)
XLA Ops:
  0.7 1.6 %shard_map.112 = (bf16[512,256]{1,0:T(8,128)(2,1)S(1)}, bf16[512,256]{1,0:T(8,128)(2,1)S(1)}, bf16[512,256]{1,0:T(8,128)(2,1)S(1)}, bf16[512,256]{1,0:T(8,128)(2,1)S(1)}) custom-call(bf16[4096,128]{1,0:T(8,128)(2,1)} %bitcast.37), custom_call_target="tpu_custom_call" | custom-call | tf_op jit(solution)/shard_map/pallas_call | solution.py:241
  2.3 4.5 %collective-permute-start = (bf16[512,256]{1,0:T(8,128)(2,1)S(1)}, bf16[512,256]{1,0:T(8,128)(2,1)S(1)}, u32[]{:S(2)}, u32[]{:S(2)}) collective-permute-start(bf16[512,256]{1,0:T(8,128)(2,1)S(1)} %get-tuple-element.18), channel_id=1, source_target_pairs={{0,2},{1,3},{2,4},{3,5},{4,6},{5,7},{6,0},{7,1},{8,14},{9,15},{10,... | collective-permute-start | bytes 786440 | tf_op jit(solution)/shard_map/ppermute | solution.py:222
  6.8 3.5 %collective-permute-start.1 = (bf16[512,256]{1,0:T(8,128)(2,1)S(1)}, bf16[512,256]{1,0:T(8,128)(2,1)S(1)}, u32[]{:S(2)}, u32[]{:S(2)}) collective-permute-start(bf16[512,256]{1,0:T(8,128)(2,1)S(1)} %get-tuple-element.19), channel_id=1, source_target_pairs={{0,1},{1,2},{2,3},{3,4},{4,5},{5,6},{6,7},{7,0},{8,15},{9,8},{10,9... | collective-permute-start | bytes 786440 | tf_op jit(solution)/shard_map/ppermute | solution.py:222
  10.3 3.6 %collective-permute-start.2 = (bf16[512,256]{1,0:T(8,128)(2,1)S(1)}, bf16[512,256]{1,0:T(8,128)(2,1)S(1)}, u32[]{:S(2)}, u32[]{:S(2)}) collective-permute-start(bf16[512,256]{1,0:T(8,128)(2,1)S(1)} %get-tuple-element.20), channel_id=1, source_target_pairs={{0,7},{1,0},{2,1},{3,2},{4,3},{5,4},{6,5},{7,6},{8,9},{9,10},{10,1... | collective-permute-start | bytes 786440 | tf_op jit(solution)/shard_map/ppermute | solution.py:222
  13.9 0.1 copy.14
  14.0 0.1 reshape.133
  14.1 0.2 dynamic-slice_reduce_fusion
  14.3 0.6 gather_fusion
  15.0 0.6 gather_fusion.1
  15.6 0.1 and_convert_fusion.gather_ref
  15.8 0.6 fusion.1
  16.4 3.7 %collective-permute-done.1.one_ref = bf16[512,256]{1,0:T(8,128)(2,1)S(1)} collective-permute-done((bf16[512,256]{1,0:T(8,128)(2,1)S(1)}, bf16[512,256]{1,0:T(8,128)(2,1)S(1)}, u32[]{:S(2)}, u32[]{:S(2)}) %collective-permute-start.1) | collective-permute-done | bytes 262176 | tf_op jit(solution)/shard_map/ppermute | solution.py:222
  20.1 0.5 shard_map.113
  20.6 41.8 %all_to_all.22 = bf16[512,4,128]{2,1,0:T(4,128)(2,1)S(1)} all-to-all(bf16[512,4,128]{2,1,0:T(4,128)(2,1)S(1)} %bitcast.28), channel_id=1, replica_groups=mesh['fsdp'=64,'rep'=8] {'fsdp','rep'}, dimensions={0} | all-to-all | bytes 1048576 | tf_op jit(solution)/shard_map/all_to_all | solution.py:225
  62.5 2.0 %shard_map.114 = (bf16[2,256,256]{2,1,0:T(8,128)(2,1)S(1)}, bf16[2048,128]{1,0:T(8,128)(2,1)S(1)}) custom-call(s32[2,2]{1,0:T(2,128)S(1)} %pad_add_fusion.limits_ref, bf16[256,512]{1,0:T(8,128)(2,1)S(1)} %and_convert_fusion.gather_ref, bf16[2048,128]{1,0:T(8,128)(2,1)S(1)} %bitcast.29, bf16[2,256,256]{2,1,0:T(8,128)(2,1)S(1)} %bitcast.35, ...), custom_call_target="tpu_custom_call" | custom-call | tf_op jit(solution)/shard_map/pallas_call | solution.py:268
  64.5 31.7 %all_to_all.23 = bf16[512,4,128]{2,1,0:T(4,128)(2,1)S(1)} all-to-all(bf16[512,4,128]{2,1,0:T(4,128)(2,1)S(1)} %bitcast.34), channel_id=1, replica_groups=mesh['fsdp'=64,'rep'=8] {'fsdp','rep'}, dimensions={0} | all-to-all | bytes 1048576 | tf_op jit(solution)/shard_map/all_to_all | solution.py:225
  96.2 0.5 shard_map.115.refs_0_
  96.7 2.9 %collective-permute-start.3 = (bf16[512,256]{1,0:T(8,128)(2,1)S(1)}, bf16[512,256]{1,0:T(8,128)(2,1)S(1)}, u32[]{:S(2)}, u32[]{:S(2)}) collective-permute-start(bf16[512,256]{1,0:T(8,128)(2,1)S(1)} %shard_map.115.refs_0_), channel_id=1, source_target_pairs={{0,2},{1,3},{2,4},{3,5},{4,6},{5,7},{6,0},{7,1},{8,14},{9,15},{10,... | collective-permute-start | bytes 786440 | tf_op jit(solution)/shard_map/ppermute | solution.py:222
  99.6 4.4 %collective-permute-start.4 = (bf16[512,256]{1,0:T(8,128)(2,1)S(1)}, bf16[512,256]{1,0:T(8,128)(2,1)S(1)}, u32[]{:S(2)}, u32[]{:S(2)}) collective-permute-start(bf16[512,256]{1,0:T(8,128)(2,1)S(1)} %shard_map.115.refs_0_), channel_id=1, source_target_pairs={{0,7},{1,0},{2,1},{3,2},{4,3},{5,4},{6,5},{7,6},{8,9},{9,10},{10,1... | collective-permute-start | bytes 786440 | tf_op jit(solution)/shard_map/ppermute | solution.py:222
  104.1 1.9 %collective-permute-start.5 = (bf16[512,256]{1,0:T(8,128)(2,1)S(1)}, bf16[512,256]{1,0:T(8,128)(2,1)S(1)}, u32[]{:S(2)}, u32[]{:S(2)}) collective-permute-start(bf16[512,256]{1,0:T(8,128)(2,1)S(1)} %shard_map.115.refs_0_), channel_id=1, source_target_pairs={{0,1},{1,2},{2,3},{3,4},{4,5},{5,6},{6,7},{7,0},{8,15},{9,8},{10,9... | collective-permute-start | bytes 786440 | tf_op jit(solution)/shard_map/ppermute | solution.py:222
  106.0 6.3 %collective-permute-done.3.refs_1_ = bf16[512,256]{1,0:T(8,128)(2,1)S(1)} collective-permute-done((bf16[512,256]{1,0:T(8,128)(2,1)S(1)}, bf16[512,256]{1,0:T(8,128)(2,1)S(1)}, u32[]{:S(2)}, u32[]{:S(2)}) %collective-permute-start.3) | collective-permute-done | bytes 262176 | tf_op jit(solution)/shard_map/ppermute | solution.py:222
  112.3 1.3 %shard_map.117 = (f32[2,256,256]{2,1,0:T(8,128)}, f32[2,256,256]{2,1,0:T(8,128)}) custom-call(bf16[2,256,256]{2,1,0:T(8,128)(2,1)S(1)} %get-tuple-element.27.grad_ref, f32[2,256,256]{2,1,0:T(8,128)S(1)} %bitcast.32, f32[2,256,256]{2,1,0:T(8,128)S(1)} %bitcast.33), custom_call_target="tpu_custom_call" | custom-call | tf_op jit(solution)/shard_map/pallas_call | solution.py:291
  113.6 1.3 %collective-permute-done.5.refs_3_ = bf16[512,256]{1,0:T(8,128)(2,1)S(1)} collective-permute-done((bf16[512,256]{1,0:T(8,128)(2,1)S(1)}, bf16[512,256]{1,0:T(8,128)(2,1)S(1)}, u32[]{:S(2)}, u32[]{:S(2)}) %collective-permute-start.5) | collective-permute-done | bytes 262176 | tf_op jit(solution)/shard_map/ppermute | solution.py:222
  114.9 1.4 %shard_map.116 = bf16[4096,128]{1,0:T(8,128)(2,1)} custom-call(bf16[512,256]{1,0:T(8,128)(2,1)S(1)} %shard_map.115.refs_0_, bf16[512,256]{1,0:T(8,128)(2,1)S(1)} %collective-permute-done.3.refs_1_, bf16[512,256]{1,0:T(8,128)(2,1)S(1)} %collective-permute-done.4.refs_2_, bf16[512,256]{1,0:T(8,128)(2,1)S(1)} %collective-permute-done.5.refs_3_), custom_call_target="tpu_custom_call" | custom-call | tf_op jit(solution)/shard_map/pallas_call | solution.py:298
  (25 shorter events, 0.1 us)
Async XLA Ops:
  0.6 13.7 %copy-start = (s32[512]{0:T(512)S(1)}, s32[512]{0:T(512)}, u32[]{:S(2)}) copy-start(s32[512]{0:T(512)} %param.13) | copy-start | bytes 6148
  0.6 13.3 %copy-start.7 = (s32[64,8,2]{0,2,1:T(2,128)S(1)}, s32[64,8,2]{0,2,1:T(2,128)}, u32[]{:S(2)}) copy-start(s32[64,8,2]{0,2,1:T(2,128)} %param.12) | copy-start | bytes 12292
  0.7 14.3 %copy-start.6 = (s32[512]{0:T(512)S(1)}, s32[512]{0:T(512)}, u32[]{:S(2)}) copy-start(s32[512]{0:T(512)} %param.14) | copy-start | bytes 6148
  2.3 14.1 %collective-permute-start = (bf16[512,256]{1,0:T(8,128)(2,1)S(1)}, bf16[512,256]{1,0:T(8,128)(2,1)S(1)}, u32[]{:S(2)}, u32[]{:S(2)}) collective-permute-start(bf16[512,256]{1,0:T(8,128)(2,1)S(1)} %get-tuple-element.18), channel_id=1, source_target_pairs={{0,2},{1,3},{2,4},{3,5},{4,6},{5,7},{6,0},{7,1},{8,14},{9,15},{10,... | collective-permute-start | bytes 786440 | tf_op jit(solution)/shard_map/ppermute | solution.py:222
  6.8 13.2 %collective-permute-start.1 = (bf16[512,256]{1,0:T(8,128)(2,1)S(1)}, bf16[512,256]{1,0:T(8,128)(2,1)S(1)}, u32[]{:S(2)}, u32[]{:S(2)}) collective-permute-start(bf16[512,256]{1,0:T(8,128)(2,1)S(1)} %get-tuple-element.19), channel_id=1, source_target_pairs={{0,1},{1,2},{2,3},{3,4},{4,5},{5,6},{6,7},{7,0},{8,15},{9,8},{10,9... | collective-permute-start | bytes 786440 | tf_op jit(solution)/shard_map/ppermute | solution.py:222
  10.3 9.7 %collective-permute-start.2 = (bf16[512,256]{1,0:T(8,128)(2,1)S(1)}, bf16[512,256]{1,0:T(8,128)(2,1)S(1)}, u32[]{:S(2)}, u32[]{:S(2)}) collective-permute-start(bf16[512,256]{1,0:T(8,128)(2,1)S(1)} %get-tuple-element.20), channel_id=1, source_target_pairs={{0,7},{1,0},{2,1},{3,2},{4,3},{5,4},{6,5},{7,6},{8,9},{9,10},{10,1... | collective-permute-start | bytes 786440 | tf_op jit(solution)/shard_map/ppermute | solution.py:222
  20.6 41.9 %copy-start.1 = (f32[1,1,2,256,256]{4,3,2,1,0:T(8,128)S(1)}, f32[1,1,2,256,256]{4,3,2,1,0:T(8,128)}, u32[]{:S(2)}) copy-start(f32[1,1,2,256,256]{4,3,2,1,0:T(8,128)} %param.19) | copy-start | bytes 1572868
  20.6 41.9 %copy-start.4 = (bf16[1,1,2,256,256]{4,3,2,1,0:T(8,128)(2,1)S(1)}, bf16[1,1,2,256,256]{4,3,2,1,0:T(8,128)(2,1)}, u32[]{:S(2)}) copy-start(bf16[1,1,2,256,256]{4,3,2,1,0:T(8,128)(2,1)} %param.17) | copy-start | bytes 786436
  20.6 41.9 %copy-start.5 = (bf16[1,1,2,256,256]{4,3,2,1,0:T(8,128)(2,1)S(1)}, bf16[1,1,2,256,256]{4,3,2,1,0:T(8,128)(2,1)}, u32[]{:S(2)}) copy-start(bf16[1,1,2,256,256]{4,3,2,1,0:T(8,128)(2,1)} %param.18) | copy-start | bytes 786436
  96.2 16.1 %copy-start.2 = (f32[1,1,2,256,256]{4,3,2,1,0:T(8,128)S(1)}, f32[1,1,2,256,256]{4,3,2,1,0:T(8,128)}, u32[]{:S(2)}) copy-start(f32[1,1,2,256,256]{4,3,2,1,0:T(8,128)} %param.15) | copy-start | bytes 1572868
  96.2 16.1 %copy-start.3 = (f32[1,1,2,256,256]{4,3,2,1,0:T(8,128)S(1)}, f32[1,1,2,256,256]{4,3,2,1,0:T(8,128)}, u32[]{:S(2)}) copy-start(f32[1,1,2,256,256]{4,3,2,1,0:T(8,128)} %param.16) | copy-start | bytes 1572868
  96.7 15.6 %collective-permute-start.3 = (bf16[512,256]{1,0:T(8,128)(2,1)S(1)}, bf16[512,256]{1,0:T(8,128)(2,1)S(1)}, u32[]{:S(2)}, u32[]{:S(2)}) collective-permute-start(bf16[512,256]{1,0:T(8,128)(2,1)S(1)} %shard_map.115.refs_0_), channel_id=1, source_target_pairs={{0,2},{1,3},{2,4},{3,5},{4,6},{5,7},{6,0},{7,1},{8,14},{9,15},{10,... | collective-permute-start | bytes 786440 | tf_op jit(solution)/shard_map/ppermute | solution.py:222
  99.6 13.9 %collective-permute-start.4 = (bf16[512,256]{1,0:T(8,128)(2,1)S(1)}, bf16[512,256]{1,0:T(8,128)(2,1)S(1)}, u32[]{:S(2)}, u32[]{:S(2)}) collective-permute-start(bf16[512,256]{1,0:T(8,128)(2,1)S(1)} %shard_map.115.refs_0_), channel_id=1, source_target_pairs={{0,7},{1,0},{2,1},{3,2},{4,3},{5,4},{6,5},{7,6},{8,9},{9,10},{10,1... | collective-permute-start | bytes 786440 | tf_op jit(solution)/shard_map/ppermute | solution.py:222
  104.1 10.8 %collective-permute-start.5 = (bf16[512,256]{1,0:T(8,128)(2,1)S(1)}, bf16[512,256]{1,0:T(8,128)(2,1)S(1)}, u32[]{:S(2)}, u32[]{:S(2)}) collective-permute-start(bf16[512,256]{1,0:T(8,128)(2,1)S(1)} %shard_map.115.refs_0_), channel_id=1, source_target_pairs={{0,1},{1,2},{2,3},{3,4},{4,5},{5,6},{6,7},{7,0},{8,15},{9,8},{10,9... | collective-permute-start | bytes 786440 | tf_op jit(solution)/shard_map/ppermute | solution.py:222
